TPU v7x, 128 devices: a whole 4x4x4 slice. The times are simulated.
128 devices in a mesh: dp: 16 (over z, y), ctx: 8 (over x, core).
Axes of the slice: x: 4, y: 4, z: 4, core: 2. Of those that a mesh axis runs over, the one named last changes fastest.
Arguments:
- queries: bfloat16 [16384, 4096], P(('dp', 'ctx')), may hold values from -40 to 40
- loader_key_rows: bfloat16 [16384, 512], P(('dp', 'ctx')), may hold values from -40 to 40
- loader_value_rows: bfloat16 [16384, 512], P(('dp', 'ctx')), may hold values from -6 to 6
- output_gradient: bfloat16 [16384, 4096], P(('dp', 'ctx')), may hold values from -6 to 6
- packing: int32 [128, 128], P(('dp', 'ctx')), may hold values from 0 to 127, each once within a row
- documents: int32 [16, 1024], P('dp'), may hold values from 0 to 3, never falling along the last dimension, each value on 1 to 512 neighbouring positions
Outputs:
- attn_out: bfloat16 [16384, 4096], P(('dp', 'ctx'))
- grad_queries: float32 [16384, 4096], P(('dp', 'ctx'))
- key_gradients: float32 [16384, 512], P(('dp', 'ctx'))
- value_gradients: float32 [16384, 512], P(('dp', 'ctx'))
Inputs may be any that keep to these rules, and one draw needn't show every extreme that they name: `packing`: each row holds every number of 0 to 127 once. `documents`: ids never fall along a sequence; each document has 1 to 512 positions, one exactly 512.
All inputs are finite; a program needn't handle non-finite values.
Results may differ from a plain program's by a relative error of at most 0.04.
Values may be sent and summed in bfloat16 or wider, within the bound.
A program may use at most 64 MiB of HBM per device.

v0:
```python
import math

import jax
import jax.numpy as jnp
from jax import lax
from jax.sharding import PartitionSpec as P

QUERY_HEADS = 32
KEY_HEADS = 4
HEAD_WIDTH = 128
QUERY_PER_KEY = 8


def keep_carry(carry_in):
    return carry_in


def local(queries, loader_key_rows, loader_value_rows, output_gradient, packing, documents):
    count_of_rows = queries.shape[0]
    device_count = lax.axis_size(("dp", "ctx"))
    context_count = lax.axis_size("ctx")
    seq_count = device_count // context_count
    slot_rows = count_of_rows // device_count
    halved_rows = count_of_rows // 2
    scale = 1.0 / math.sqrt(HEAD_WIDTH)
    my_device = lax.axis_index(("dp", "ctx"))
    my_column = lax.axis_index("ctx")

    def block_of(column, upper):
        return jnp.where(upper, column, column)

    shape_grid = (seq_count, context_count, slot_rows)
    seq_index = lax.broadcasted_iota(jnp.int32, shape_grid, 0)
    col_index = lax.broadcasted_iota(jnp.int32, shape_grid, 1)
    slot_index = lax.broadcasted_iota(jnp.int32, shape_grid, 2)
    my_upper = my_device >= device_count // 2
    wanted = (seq_index * context_count + block_of(col_index, my_upper)) * slot_rows + slot_index
    picks = jnp.take(packing[0], wanted.reshape(-1), axis=0)
    sent_query = jnp.take(queries, picks, axis=0)
    sent_key = jnp.take(loader_key_rows, picks, axis=0)
    sent_value = jnp.take(loader_value_rows, picks, axis=0)
    sent_grad = jnp.take(output_gradient, picks, axis=0)
    received_query, recv_key, recv_value, received_gradient = (
        lax.all_to_all(sent_query, ("dp", "ctx"), split_axis=0, concat_axis=0, tiled=True),
        lax.all_to_all(sent_key, ("dp", "ctx"), split_axis=0, concat_axis=0, tiled=True),
        lax.all_to_all(sent_value, ("dp", "ctx"), split_axis=0, concat_axis=0, tiled=True),
        lax.all_to_all(sent_grad, ("dp", "ctx"), split_axis=0, concat_axis=0, tiled=True),
    )
    row_iota = jnp.arange(count_of_rows, dtype=jnp.int32)
    source_upper = row_iota // slot_rows >= device_count // 2
    query_pos = block_of(my_column, source_upper) * count_of_rows + row_iota
    doc_line = documents[0]
    query_doc = jnp.take(doc_line, query_pos)
    whole_key, whole_value = (
        lax.all_gather(recv_key, "ctx", axis=0, tiled=True),
        lax.all_gather(recv_value, "ctx", axis=0, tiled=True),
    )
    grouped_query_heads = received_query.reshape(
        count_of_rows, KEY_HEADS, QUERY_PER_KEY, HEAD_WIDTH
    )
    gradient_heads = received_gradient.reshape(count_of_rows, KEY_HEADS, QUERY_PER_KEY, HEAD_WIDTH)

    def shard_blocks(shard):
        start = shard * count_of_rows
        key_block = lax.dynamic_slice_in_dim(whole_key, start, count_of_rows, 0).reshape(
            count_of_rows, KEY_HEADS, HEAD_WIDTH
        )
        value_block = lax.dynamic_slice_in_dim(whole_value, start, count_of_rows, 0).reshape(
            count_of_rows, KEY_HEADS, HEAD_WIDTH
        )
        return (key_block, value_block)

    def shard_mask(shard, pos_half, doc_half):
        key_pos = block_of(shard, source_upper) * count_of_rows + row_iota
        key_doc = jnp.take(doc_line, key_pos)
        return (key_pos[None, :] <= pos_half[:, None]) & (key_doc[None, :] == doc_half[:, None])

    key_gradient_total = jnp.zeros(
        (context_count * count_of_rows, KEY_HEADS, HEAD_WIDTH), jnp.float32
    )
    value_gradient_total = jnp.zeros(
        (context_count * count_of_rows, KEY_HEADS, HEAD_WIDTH), jnp.float32
    )
    out_parts = []
    grad_query_parts = []
    for half_index in range(2):
        lower = half_index * halved_rows
        query_half = grouped_query_heads[lower : lower + halved_rows]
        grad_half = gradient_heads[lower : lower + halved_rows]
        pos_half = query_pos[lower : lower + halved_rows]
        doc_half = query_doc[lower : lower + halved_rows]

        def scores_of(key_block):
            return (
                jnp.einsum(
                    "qgrd,kgd->grqk", query_half, key_block, preferred_element_type=jnp.float32
                )
                * scale
            )

        def stats_step(shard, carry):
            causal_mask = shard_mask(shard, pos_half, doc_half)

            def live_stats(carry_in):
                best, total = carry_in
                key_block, value_block = shard_blocks(shard)
                masked = jnp.where(causal_mask, scores_of(key_block), -1e30)
                new_best = jnp.maximum(best, jnp.max(masked, axis=-1))
                added = jnp.sum(
                    jnp.where(causal_mask, jnp.exp(masked - new_best[..., None]), 0.0), axis=-1
                )
                return (new_best, total * jnp.exp(best - new_best) + added)

            return lax.cond(jnp.any(causal_mask), live_stats, keep_carry, carry)

        initial_maximum = jnp.full((KEY_HEADS, QUERY_PER_KEY, halved_rows), -1e30, jnp.float32)
        best, total = lax.fori_loop(
            0, context_count, stats_step, (initial_maximum, jnp.zeros_like(initial_maximum))
        )
        log_sum = best + jnp.log(total)

        def output_update(shard, carry):
            causal_mask = shard_mask(shard, pos_half, doc_half)

            def live_output(carry_in):
                key_block, value_block = shard_blocks(shard)
                probs = jnp.where(
                    causal_mask, jnp.exp(scores_of(key_block) - log_sum[..., None]), 0.0
                ).astype(jnp.bfloat16)
                return carry_in + jnp.einsum(
                    "grqk,kgd->qgrd", probs, value_block, preferred_element_type=jnp.float32
                )

            return lax.cond(jnp.any(causal_mask), live_output, keep_carry, carry)

        accum = lax.fori_loop(
            0,
            context_count,
            output_update,
            jnp.zeros((halved_rows, KEY_HEADS, QUERY_PER_KEY, HEAD_WIDTH), jnp.float32),
        )
        out_half = accum.astype(jnp.bfloat16)
        delta = jnp.transpose(
            jnp.sum(out_half.astype(jnp.float32) * grad_half.astype(jnp.float32), axis=-1),
            (1, 2, 0),
        )

        def backward_step(shard, carry):
            causal_mask = shard_mask(shard, pos_half, doc_half)

            def live_backward(carry_in):
                grad_query, grad_key_acc, grad_value_acc = carry_in
                key_block, value_block = shard_blocks(shard)
                probs = jnp.where(
                    causal_mask, jnp.exp(scores_of(key_block) - log_sum[..., None]), 0.0
                )
                probs_b = probs.astype(jnp.bfloat16)
                dprob = jnp.einsum(
                    "qgrd,kgd->grqk", grad_half, value_block, preferred_element_type=jnp.float32
                )
                dscore = (probs * (dprob - delta[..., None]) * scale).astype(jnp.bfloat16)
                grad_query = grad_query + jnp.einsum(
                    "grqk,kgd->qgrd", dscore, key_block, preferred_element_type=jnp.float32
                )
                key_term = jnp.einsum(
                    "grqk,qgrd->kgd", dscore, query_half, preferred_element_type=jnp.float32
                )
                value_term = jnp.einsum(
                    "grqk,qgrd->kgd", probs_b, grad_half, preferred_element_type=jnp.float32
                )
                start = shard * count_of_rows
                old_key = lax.dynamic_slice_in_dim(grad_key_acc, start, count_of_rows, 0)
                old_value = lax.dynamic_slice_in_dim(grad_value_acc, start, count_of_rows, 0)
                grad_key_acc = lax.dynamic_update_slice_in_dim(
                    grad_key_acc, old_key + key_term, start, 0
                )
                grad_value_acc = lax.dynamic_update_slice_in_dim(
                    grad_value_acc, old_value + value_term, start, 0
                )
                return (grad_query, grad_key_acc, grad_value_acc)

            return lax.cond(jnp.any(causal_mask), live_backward, keep_carry, carry)

        initial_gradient = jnp.zeros(
            (halved_rows, KEY_HEADS, QUERY_PER_KEY, HEAD_WIDTH), jnp.float32
        )
        grad_query, key_gradient_total, value_gradient_total = lax.fori_loop(
            0,
            context_count,
            backward_step,
            (initial_gradient, key_gradient_total, value_gradient_total),
        )
        out_parts.append(out_half.reshape(halved_rows, QUERY_HEADS * HEAD_WIDTH))
        grad_query_parts.append(grad_query.reshape(halved_rows, QUERY_HEADS * HEAD_WIDTH))
    local_key, local_value = (
        lax.psum_scatter(key_gradient_total, "ctx", scatter_dimension=0, tiled=True),
        lax.psum_scatter(value_gradient_total, "ctx", scatter_dimension=0, tiled=True),
    )
    out_rows = jnp.concatenate(out_parts, axis=0).astype(jnp.float32)
    grad_query_rows = jnp.concatenate(grad_query_parts, axis=0)
    key_gradient_rows = local_key.reshape(count_of_rows, KEY_HEADS * HEAD_WIDTH)
    value_gradient_rows = local_value.reshape(count_of_rows, KEY_HEADS * HEAD_WIDTH)
    back_out, back_query, back_key, back_value = (
        lax.all_to_all(out_rows, ("dp", "ctx"), split_axis=0, concat_axis=0, tiled=True),
        lax.all_to_all(grad_query_rows, ("dp", "ctx"), split_axis=0, concat_axis=0, tiled=True),
        lax.all_to_all(key_gradient_rows, ("dp", "ctx"), split_axis=0, concat_axis=0, tiled=True),
        lax.all_to_all(value_gradient_rows, ("dp", "ctx"), split_axis=0, concat_axis=0, tiled=True),
    )
    attn_out = jnp.zeros_like(queries).at[picks].set(back_out.astype(jnp.bfloat16))
    grad_queries = jnp.zeros(queries.shape, jnp.float32).at[picks].set(back_query)
    key_gradients = jnp.zeros(loader_key_rows.shape, jnp.float32).at[picks].set(back_key)
    value_gradients = jnp.zeros(loader_value_rows.shape, jnp.float32).at[picks].set(back_value)
    return (attn_out, grad_queries, key_gradients, value_gradients)


def solution(mesh):
    in_specs = (
        P(("dp", "ctx"), None),
        P(("dp", "ctx"), None),
        P(("dp", "ctx"), None),
        P(("dp", "ctx"), None),
        P(("dp", "ctx"), None),
        P("dp", None),
    )
    out_specs = (
        P(("dp", "ctx"), None),
        P(("dp", "ctx"), None),
        P(("dp", "ctx"), None),
        P(("dp", "ctx"), None),
    )
    return jax.shard_map(local, mesh=mesh, in_specs=in_specs, out_specs=out_specs, check_vma=False)
```

profile of v0, /device:TPU:1, one launch (start us, length us, event | category | flops | bytes accessed | tf_op | source)
XLA Modules:
  0.0 478.6 jit_solution(12722757358338200964)
XLA Ops:
  7.7 1.6 gather_fusion.6
  9.3 1.8 gather_fusion.8
  13.9 11.5 %all-to-all-start.1 = ((bf16[128,2,256]{2,1,0:T(2,128)(2,1)}), bf16[128,2,256]{2,1,0:T(2,128)(2,1)S(1)}, u32[]{:S(2)}, u32[]{:S(2)}) async-start(bf16[128,2,256]{2,1,0:T(2,128)(2,1)} %reshape.455), calls=%async_computation.1 | async-start | bytes 262144 | tf_op jit(solution)/shard_map/all_to_all | solution.py:45
  29.2 6.2 %all-to-all-done.1 = bf16[128,2,256]{2,1,0:T(2,128)(2,1)S(1)} async-done(((bf16[128,2,256]{2,1,0:T(2,128)(2,1)}), bf16[128,2,256]{2,1,0:T(2,128)(2,1)S(1)}, u32[]{:S(2)}, u32[]{:S(2)}) %all-to-all-start.1) | async-done | bytes 131104 | tf_op jit(solution)/shard_map/all_to_all | solution.py:45
  35.5 4.2 all-to-all-start
  41.8 2.6 reduce.11
  44.4 1.6 reshape.457
  46.0 3.8 all-to-all-done
  49.7 6.0 %all-to-all-start.2 = ((bf16[128,2,2048]{2,1,0:T(2,128)(2,1)}), bf16[128,2,2048]{2,1,0:T(2,128)(2,1)S(1)}, u32[]{:S(2)}, u32[]{:S(2)}) async-start(bf16[128,2,2048]{2,1,0:T(2,128)(2,1)} %reshape.457), calls=%async_computation.2 | async-start | bytes 2097152 | tf_op jit(solution)/shard_map/all_to_all | solution.py:44
  55.7 1.4 reduce.8
  57.1 1.6 reshape.459
  59.7 18.3 %all-to-all-done.2 = bf16[128,2,2048]{2,1,0:T(2,128)(2,1)S(1)} async-done(((bf16[128,2,2048]{2,1,0:T(2,128)(2,1)}), bf16[128,2,2048]{2,1,0:T(2,128)(2,1)S(1)}, u32[]{:S(2)}, u32[]{:S(2)}) %all-to-all-start.2) | async-done | bytes 1048608 | tf_op jit(solution)/shard_map/all_to_all | solution.py:44
  78.0 5.2 %all-to-all-start.4 = ((bf16[128,2,2048]{2,1,0:T(2,128)(2,1)}), bf16[128,2,2048]{2,1,0:T(2,128)(2,1)}, u32[]{:S(2)}, u32[]{:S(2)}) async-start(bf16[128,2,2048]{2,1,0:T(2,128)(2,1)} %reshape.459), calls=%async_computation.4 | async-start | bytes 2097152 | tf_op jit(solution)/shard_map/all_to_all | solution.py:47
  85.5 5.4 %slice_reduce_fusion.3 = (bf16[64,4096]{1,0:T(8,128)(2,1)S(1)}, bf16[64,4096]{1,0:T(8,128)(2,1)}) fusion(bf16[128,1,4096]{2,1,0:T(2,128)(2,1)S(1)} %reshape.458), kind=kLoop, calls=%fused_computation.150 | loop fusion | bytes 2097152 | tf_op jit(solution)/shard_map/slice | solution.py:88
  91.3 11.1 %all-to-all-done.4 = bf16[128,2,2048]{2,1,0:T(2,128)(2,1)} async-done(((bf16[128,2,2048]{2,1,0:T(2,128)(2,1)}), bf16[128,2,2048]{2,1,0:T(2,128)(2,1)}, u32[]{:S(2)}, u32[]{:S(2)}) %all-to-all-start.4) | async-done | bytes 1048608 | tf_op jit(solution)/shard_map/all_to_all | solution.py:47
  102.4 7.5 %reshape.460 = bf16[128,1,4096]{2,1,0:T(2,128)(2,1)} reshape(bf16[128,2,2048]{2,1,0:T(2,128)(2,1)} %all-to-all-done.4) | data formatting | bytes 2097152
  109.9 5.8 %slice_reduce_fusion = (bf16[64,4096]{1,0:T(8,128)(2,1)S(1)}, bf16[64,4096]{1,0:T(8,128)(2,1)S(1)}) fusion(bf16[128,1,4096]{2,1,0:T(2,128)(2,1)} %reshape.460), kind=kLoop, calls=%fused_computation.147 | loop fusion | bytes 2097152 | tf_op jit(solution)/shard_map/slice | solution.py:89
  118.0 1.5 copy.239
  119.5 22.0 %while.102 = (s32[]{:T(128)}, f32[4,8,64]{2,1,0:T(8,128)S(1)}, f32[4,8,64]{2,1,0:T(8,128)S(1)}, s32[64]{0:T(128)S(1)}, s32[1024]{0:T(1024)S(1)}, /*index=5*/s32[...) while((s32[]{:T(128)}, f32[4,8,64]{2,1,0:T(8,128)S(1)}, ...), condition=%wide.region_6.10_spmd.clone, body=%wide.region_0.9_spmd.clone.sunk | while | flops 68721152 | bytes 3155721 | solution.py:117
  141.6 2.6 copy.238
  144.3 23.0 %while.103 = (s32[]{:T(128)}, f32[64,4,8,128]{3,0,2,1:T(8,128)S(1)}, s32[64]{0:T(128)S(1)}, s32[1024]{0:T(1024)S(1)}, s32[64]{0:T(128)S(1)}, /*index=5*/bf16[102...) while((s32[]{:T(128)}, f32[64,4,8,128]{3,0,2,1:T(8,128)S(1)}, ...), condition=%wide.region_11.15_spmd.clone, body=%wide.region_7.14_spmd.clone.sunk | while | flops 135563776 | bytes 3442425 | solution.py:136
  146.7 1.8 conditional.19
  150.9 1.8 conditional.19
  167.3 2.6 multiply_reduce_fusion.1
  170.0 1.5 broadcast.272
  171.4 1.5 broadcast.272.clone
  173.1 31.9 %while.106 = (s32[]{:T(128)}, f32[64,4,8,128]{3,0,2,1:T(8,128)S(1)}, f32[1024,4,128]{2,0,1:T(8,128)}, f32[1024,4,128]{2,0,1:T(8,128)}, s32[64]{0:T(128)S(1)}, /*...) while((s32[]{:T(128)}, f32[64,4,8,128]{3,0,2,1:T(8,128)S(1)}, ...), condition=%wide.region_30.34_spmd.clone, body=%wide.region_26.33_spmd.clone.sunk | while | flops 338070016 | bytes 10921841 | solution.py:187
  175.7 6.2 %conditional.22 = ((f32[64,4,8,128]{3,0,2,1:T(8,128)S(1)}, f32[1024,4,128]{2,0,1:T(8,128)}, f32[1024,4,128]{2,0,1:T(8,128)})) conditional(s32[]{:T(128)} %convert_element_type.142, (f32[64,4,8,128]{3,0,2,1:T(8,128)S(1)}, f32[1024,4,128]{2,0,1:T(8,128)}, f32[1024,4,128]{2,0,1:T(8,128)}) %tuple.331, (s32[]{:T(128)}, bf16[1024,512]{0,1:T(8,128)(2,1)}, ...), branch_computations={%region_28.31_spmd, %region_29.32_spmd} | conditional | flops 338034688 | bytes 10903642 | solution.py:182
  177.5 2.0 fusion.50
  179.8 2.0 fusion.52
  184.2 6.2 %conditional.22 = ((f32[64,4,8,128]{3,0,2,1:T(8,128)S(1)}, f32[1024,4,128]{2,0,1:T(8,128)}, f32[1024,4,128]{2,0,1:T(8,128)})) conditional(s32[]{:T(128)} %convert_element_type.142, (f32[64,4,8,128]{3,0,2,1:T(8,128)S(1)}, f32[1024,4,128]{2,0,1:T(8,128)}, f32[1024,4,128]{2,0,1:T(8,128)}) %tuple.331, (s32[]{:T(128)}, bf16[1024,512]{0,1:T(8,128)(2,1)}, ...), branch_computations={%region_28.31_spmd, %region_29.32_spmd} | conditional | flops 338034688 | bytes 10903642 | solution.py:182
  186.0 2.0 fusion.50
  188.4 2.0 fusion.52
  205.0 23.7 %while.104 = (s32[]{:T(128)}, f32[4,8,64]{2,1,0:T(8,128)S(1)}, f32[4,8,64]{2,1,0:T(8,128)S(1)}, s32[64]{0:T(128)S(1)}, s32[1024]{0:T(1024)S(1)}, /*index=5*/s32[...) while((s32[]{:T(128)}, f32[4,8,64]{2,1,0:T(8,128)S(1)}, ...), condition=%wide.region_18.22_spmd.clone, body=%wide.region_12.21_spmd.clone.sunk | while | flops 68721152 | bytes 3155721 | solution.py:117
  207.4 2.2 conditional.20
  212.0 2.2 conditional.20
  228.9 23.0 %while.105 = (s32[]{:T(128)}, f32[64,4,8,128]{3,0,2,1:T(8,128)S(1)}, s32[64]{0:T(128)S(1)}, s32[1024]{0:T(1024)S(1)}, s32[64]{0:T(128)S(1)}, /*index=5*/bf16[102...) while((s32[]{:T(128)}, f32[64,4,8,128]{3,0,2,1:T(8,128)S(1)}, ...), condition=%wide.region_23.27_spmd.clone, body=%wide.region_19.26_spmd.clone.sunk | while | flops 135563776 | bytes 3442425 | solution.py:136
  231.3 1.8 conditional.21
  235.5 1.8 conditional.21
  251.8 2.6 multiply_reduce_fusion
  254.7 31.7 %while.107 = (s32[]{:T(128)}, f32[64,4,8,128]{3,0,2,1:T(8,128)S(1)}, f32[1024,4,128]{2,0,1:T(8,128)}, f32[1024,4,128]{2,0,1:T(8,128)}, s32[64]{0:T(128)S(1)}, /*...) while((s32[]{:T(128)}, f32[64,4,8,128]{3,0,2,1:T(8,128)S(1)}, ...), condition=%wide.region_36.40_spmd.clone, body=%wide.region_32.39_spmd.clone.sunk | while | flops 338070016 | bytes 10921841 | solution.py:187
  257.1 6.2 %conditional.23 = ((f32[64,4,8,128]{3,0,2,1:T(8,128)S(1)}, f32[1024,4,128]{2,0,1:T(8,128)}, f32[1024,4,128]{2,0,1:T(8,128)})) conditional(s32[]{:T(128)} %convert_element_type.143, (f32[64,4,8,128]{3,0,2,1:T(8,128)S(1)}, f32[1024,4,128]{2,0,1:T(8,128)}, f32[1024,4,128]{2,0,1:T(8,128)}) %tuple.336, (s32[]{:T(128)}, bf16[1024,512]{0,1:T(8,128)(2,1)}, ...), branch_computations={%region_34.37_spmd, %region_35.38_spmd} | conditional | flops 338034688 | bytes 10903642 | solution.py:182
  258.9 2.0 fusion.64
  261.2 2.0 fusion.66
  265.6 6.2 %conditional.23 = ((f32[64,4,8,128]{3,0,2,1:T(8,128)S(1)}, f32[1024,4,128]{2,0,1:T(8,128)}, f32[1024,4,128]{2,0,1:T(8,128)})) conditional(s32[]{:T(128)} %convert_element_type.143, (f32[64,4,8,128]{3,0,2,1:T(8,128)S(1)}, f32[1024,4,128]{2,0,1:T(8,128)}, f32[1024,4,128]{2,0,1:T(8,128)}) %tuple.336, (s32[]{:T(128)}, bf16[1024,512]{0,1:T(8,128)(2,1)}, ...), branch_computations={%region_34.37_spmd, %region_35.38_spmd} | conditional | flops 338034688 | bytes 10903642 | solution.py:182
  267.4 2.0 fusion.64
  269.8 2.0 fusion.66
  286.4 3.3 copy.264
  292.4 3.5 copy.263
  295.9 61.3 %all-to-all-start.5 = ((f32[128,1,4096]{2,1,0:T(1,128)}), f32[128,1,4096]{2,1,0:T(1,128)}, u32[]{:S(2)}, u32[]{:S(2)}) async-start(f32[128,1,4096]{2,1,0:T(1,128)} %copy.263), calls=%async_computation.5 | async-start | bytes 4194304 | tf_op jit(solution)/shard_map/all_to_all | solution.py:205
  357.2 1.9 copy.266
  360.8 3.5 copy.248
  364.3 29.5 %all-to-all-done.5 = f32[128,1,4096]{2,1,0:T(1,128)} async-done(((f32[128,1,4096]{2,1,0:T(1,128)}), f32[128,1,4096]{2,1,0:T(1,128)}, u32[]{:S(2)}, u32[]{:S(2)}) %all-to-all-start.5) | async-done | bytes 2097184 | tf_op jit(solution)/shard_map/all_to_all | solution.py:205
  393.9 4.4 all-to-all-start.3
  398.3 1.8 copy.265
  400.1 36.6 %all-to-all-done.3 = f32[128,1,4096]{2,1,0:T(1,128)S(1)} async-done(((f32[128,1,4096]{2,1,0:T(1,128)}), f32[128,1,4096]{2,1,0:T(1,128)S(1)}, u32[]{:S(2)}, u32[]{:S(2)}) %all-to-all-start.3) | async-done | bytes 2097184 | tf_op jit(solution)/shard_map/all_to_all | solution.py:204
  436.7 5.1 %all-to-all-start.6 = ((f32[128,1,512]{2,1,0:T(1,128)}), f32[128,1,512]{2,1,0:T(1,128)S(1)}, u32[]{:S(2)}, u32[]{:S(2)}) async-start(f32[128,1,512]{2,1,0:T(1,128)} %copy.265), calls=%async_computation.7 | async-start | bytes 524288 | tf_op jit(solution)/shard_map/all_to_all | solution.py:206
  441.8 1.8 copy.267
  443.6 9.4 %all-to-all-done.6 = f32[128,1,512]{2,1,0:T(1,128)S(1)} async-done(((f32[128,1,512]{2,1,0:T(1,128)}), f32[128,1,512]{2,1,0:T(1,128)S(1)}, u32[]{:S(2)}, u32[]{:S(2)}) %all-to-all-start.6) | async-done | bytes 262176 | tf_op jit(solution)/shard_map/all_to_all | solution.py:206
  453.0 5.5 %all-to-all-start.7 = ((f32[128,1,512]{2,1,0:T(1,128)}), f32[128,1,512]{2,1,0:T(1,128)}, u32[]{:S(2)}, u32[]{:S(2)}) async-start(f32[128,1,512]{2,1,0:T(1,128)} %copy.267), calls=%async_computation.9 | async-start | bytes 524288 | tf_op jit(solution)/shard_map/all_to_all | solution.py:207
  458.5 5.5 %scatter_custom_fusion.1 = f32[128,4096]{1,0:T(8,128)} fusion(s32[128]{0:T(128)S(1)} %fusion.84, f32[128,1,4096]{2,1,0:T(1,128)} %all-to-all-done.5, f32[]{:T(128)} %constant.280.clone.1), kind=kCustom, calls=%fused_computation.139 | custom fusion | bytes 4194308 | tf_op jit(solution)/shard_map/scatter | solution.py:210
  464.0 4.1 scatter_custom_fusion
  468.1 1.7 scatter_custom_fusion.2
  469.8 2.1 scatter_custom_fusion.3
  (425 shorter events, 127.2 us)
Async XLA Ops:
  7.2 18.3 %copy-start = (bf16[128,4096]{1,0:T(8,128)(2,1)S(1)}, bf16[128,4096]{1,0:T(8,128)(2,1)}, u32[]{:S(2)}) copy-start(bf16[128,4096]{1,0:T(8,128)(2,1)} %param.36) | copy-start | bytes 3145732
  7.2 3.9 copy-start.6
  13.9 21.5 %all-to-all-start.1 = ((bf16[128,2,256]{2,1,0:T(2,128)(2,1)}), bf16[128,2,256]{2,1,0:T(2,128)(2,1)S(1)}, u32[]{:S(2)}, u32[]{:S(2)}) async-start(bf16[128,2,256]{2,1,0:T(2,128)(2,1)} %reshape.455), calls=%async_computation.1 | async-start | bytes 262144 | tf_op jit(solution)/shard_map/all_to_all | solution.py:45
  25.5 1.2 copy-start.3
  35.5 14.2 %all-to-all-start = ((bf16[128,2,256]{2,1,0:T(2,128)(2,1)}), bf16[128,2,256]{2,1,0:T(2,128)(2,1)S(1)}, u32[]{:S(2)}, u32[]{:S(2)}) async-start(bf16[128,2,256]{2,1,0:T(2,128)(2,1)} %reshape.453), calls=%async_computation | async-start | bytes 262144 | tf_op jit(solution)/shard_map/all_to_all | solution.py:46
  39.7 78.3 %all-gather.7.cloned.1.call-start = ((), (), s32[]{:S(2)}) async-start(), calls=%async_computation.13 | async-start | bytes 1179648 | tf_op jit(solution)/shard_map/all_gather | solution.py:55
  49.7 28.3 %all-to-all-start.2 = ((bf16[128,2,2048]{2,1,0:T(2,128)(2,1)}), bf16[128,2,2048]{2,1,0:T(2,128)(2,1)S(1)}, u32[]{:S(2)}, u32[]{:S(2)}) async-start(bf16[128,2,2048]{2,1,0:T(2,128)(2,1)} %reshape.457), calls=%async_computation.2 | async-start | bytes 2097152 | tf_op jit(solution)/shard_map/all_to_all | solution.py:44
  55.7 3.0 copy-start.2
  78.0 24.4 %all-to-all-start.4 = ((bf16[128,2,2048]{2,1,0:T(2,128)(2,1)}), bf16[128,2,2048]{2,1,0:T(2,128)(2,1)}, u32[]{:S(2)}, u32[]{:S(2)}) async-start(bf16[128,2,2048]{2,1,0:T(2,128)(2,1)} %reshape.459), calls=%async_computation.4 | async-start | bytes 2097152 | tf_op jit(solution)/shard_map/all_to_all | solution.py:47
  83.2 58.3 %all-gather.5.cloned.1.call-start = ((), (), s32[]{:S(2)}) async-start(), calls=%async_computation.12 | async-start | bytes 1179648 | tf_op jit(solution)/shard_map/all_gather | solution.py:56
  84.2 314.1 %reduce-scatter.3.cloned.1.call-start = ((), (), s32[]{:S(2)}) async-start(), calls=%async_computation.10 | async-start | bytes 2359296 | tf_op jit(solution)/shard_map/reduce_scatter | solution.py:196
  109.9 6.2 %copy-start.11 = (bf16[64,4096]{1,0:T(8,128)(2,1)S(1)}, bf16[64,4096]{1,0:T(8,128)(2,1)}, u32[]{:S(2)}) copy-start(bf16[64,4096]{1,0:T(8,128)(2,1)} %get-tuple-element.1952) | copy-start | bytes 1572868
  115.8 0.8 copy-start.8
  116.9 0.8 copy-start.7
  141.5 2.7 copy-start.4
  295.9 61.3 %copy-start.5 = (f32[1024,4,128]{2,0,1:T(8,128)S(1)}, f32[1024,4,128]{2,0,1:T(8,128)}, u32[]{:S(2)}) copy-start(f32[1024,4,128]{2,0,1:T(8,128)} %get-tuple-element.1404) | copy-start | bytes 6291460
  295.9 98.0 %all-to-all-start.5 = ((f32[128,1,4096]{2,1,0:T(1,128)}), f32[128,1,4096]{2,1,0:T(1,128)}, u32[]{:S(2)}, u32[]{:S(2)}) async-start(f32[128,1,4096]{2,1,0:T(1,128)} %copy.263), calls=%async_computation.5 | async-start | bytes 4194304 | tf_op jit(solution)/shard_map/all_to_all | solution.py:205
  357.2 84.6 %reduce-scatter.5.cloned.1.call-start = ((), (), s32[]{:S(2)}) async-start(), calls=%async_computation.11 | async-start | bytes 2359296 | tf_op jit(solution)/shard_map/reduce_scatter | solution.py:197
  359.1 1.0 copy-start.9
  359.1 1.3 copy-start.10
  393.9 42.8 %all-to-all-start.3 = ((f32[128,1,4096]{2,1,0:T(1,128)}), f32[128,1,4096]{2,1,0:T(1,128)S(1)}, u32[]{:S(2)}, u32[]{:S(2)}) async-start(f32[128,1,4096]{2,1,0:T(1,128)} %copy.248), calls=%async_computation.3 | async-start | bytes 4194304 | tf_op jit(solution)/shard_map/all_to_all | solution.py:204
  436.7 16.3 %all-to-all-start.6 = ((f32[128,1,512]{2,1,0:T(1,128)}), f32[128,1,512]{2,1,0:T(1,128)S(1)}, u32[]{:S(2)}, u32[]{:S(2)}) async-start(f32[128,1,512]{2,1,0:T(1,128)} %copy.265), calls=%async_computation.7 | async-start | bytes 524288 | tf_op jit(solution)/shard_map/all_to_all | solution.py:206
  453.0 16.8 %all-to-all-start.7 = ((f32[128,1,512]{2,1,0:T(1,128)}), f32[128,1,512]{2,1,0:T(1,128)}, u32[]{:S(2)}, u32[]{:S(2)}) async-start(f32[128,1,512]{2,1,0:T(1,128)} %copy.267), calls=%async_computation.9 | async-start | bytes 524288 | tf_op jit(solution)/shard_map/all_to_all | solution.py:207
  458.5 13.4 %copy-start.1 = (bf16[128,4096]{1,0:T(8,128)(2,1)S(1)}, bf16[128,4096]{1,0:T(8,128)(2,1)}, u32[]{:S(2)}) copy-start(bf16[128,4096]{1,0:T(8,128)(2,1)} %param.36) | copy-start | bytes 3145732
Sparse Core Ops, SparseCore 0:
  42.8 28.1 all-gather.6
  86.4 25.3 all-gather.4
  289.8 98.1 reduce-scatter.2
  390.3 46.4 reduce-scatter.4
where the time goes:
time: 487 us; the launch traced here: 479 us
  local copies, waits for them, and re-layouts  134 us (28%)
  waiting for transfers between devices  115 us (24%)
  starting transfers between devices  104 us (21%)
  other arithmetic  50.5 us (10%)
  loops' own time  35 us (7%)
  matrix products  25.5 us (5%)
  between operations  14.6 us (3%)
    all_to_all x1, starting transfers between devices, local(): lax.all_to_all(grad_query_rows, ('dp', 'ctx'), split_axis=0, concat_axis=...  61.3 us
    gather x48, local copies, waits for them, and re-layouts, shard_mask(): key_doc = jnp.take(doc_line, key_pos)  46.6 us
    all_to_all x1, waiting for transfers between devices, local(): lax.all_to_all(out_rows, ('dp', 'ctx'), split_axis=0, concat_axis=0, tile...  36.6 us
    all_to_all x1, waiting for transfers between devices, local(): lax.all_to_all(grad_query_rows, ('dp', 'ctx'), split_axis=0, concat_axis=...  29.5 us
    unnamed x46, local copies, waits for them, and re-layouts  22.4 us
    all_to_all x1, waiting for transfers between devices, local(): lax.all_to_all(sent_query, ('dp', 'ctx'), split_axis=0, concat_axis=0, ti...  18.3 us
    all_to_all x1, starting transfers between devices, local(): lax.all_to_all(sent_key, ('dp', 'ctx'), split_axis=0, concat_axis=0, tile...  11.5 us
    reduce_or x16, other arithmetic, output_update(): return lax.cond(jnp.any(causal_mask), live_output, keep_carry, carry)  11.5 us
  transfers between devices with their start and end apart: 12, of which 7 were waited for; matrix products, arithmetic and copies ran while one was open for 17% of the time, Pallas kernels for 0%

commit v1 on v0

v1 whole, which is shorter than its diff:
```python
import math

import jax
import jax.numpy as jnp
from jax import lax
from jax.experimental import pallas as pl
from jax.experimental.pallas import tpu as pltpu
from jax.sharding import PartitionSpec as P

HEAD_WIDTH = 128
TOK_DEV = 128
N_DP = 16
N_CTX = 8
DEVICES = N_DP * N_CTX
HEADS = 4
KEY_HEADS = 4
BLOCKS = 8
SEQ = 1024
QB = 256
DOC_MOST = 512
SCALE = 1.0 / math.sqrt(HEAD_WIDTH)
MESH = pl.DeviceIdType.MESH
F32 = jnp.float32
BF16 = jnp.bfloat16
STRIDE = 37

WINDOWS = [(max(0, QB * i - DOC_MOST), QB * (i + 1)) for i in range(SEQ // QB)]
BIAS_ROWS = [sum(b - a for a, b in WINDOWS[:i]) for i in range(len(WINDOWS) + 1)]


def shifted(device, offset):
    low = 0b0101010
    return (((device & low) + (offset & low)) ^ ((device ^ offset) & (127 - low))) & 127


def dot_nt(a, b):
    return lax.dot_general(a, b, (((1,), (1,)), ((), ())), preferred_element_type=F32)


def dot_nn(a, b):
    return jnp.dot(a, b, preferred_element_type=F32)


def wait_bytes(ref, sem):
    pltpu.make_async_copy(ref, ref, sem).wait()


def main_kernel(
    q_hbm, k_hbm, v_hbm, d_hbm, pack_hbm, docs_hbm,
    ret, retkv,
    q_in, k_in, v_in, d_in, pack, docs,
    send, recv, outb, kvsend, kvrecv, kvout, xbuf,
    scr, scr2, qs, ds, dts, ks, vs, kts, vts, dks, dvs, bias,
    load_sem, in_send, in_recv, out_send, out_recv,
    kvs_sem, kvr_sem, kvx_sem, ks_sem, kr_sem, dx_sem,
):
    my_dp = lax.axis_index("dp")
    my_ctx = lax.axis_index("ctx")
    me = my_dp * N_CTX + my_ctx
    core = my_ctx % 2
    my_key = my_ctx // 2
    half = me // 64
    sibling = {"dp": my_dp, "ctx": my_ctx + 1 - 2 * core}

    def at(device):
        return {"dp": device // N_CTX, "ctx": device % N_CTX}

    barrier = pltpu.get_barrier_semaphore()

    def greet(i, carry):
        pl.semaphore_signal(barrier, inc=1, device_id=at(shifted(me, (i * STRIDE) & 127)), device_id_type=MESH)
        return carry

    lax.fori_loop(1, DEVICES, greet, 0)

    loads = [
        pltpu.make_async_copy(src, dst, load_sem.at[i])
        for i, (src, dst) in enumerate(
            ((pack_hbm, pack), (k_hbm, k_in), (v_hbm, v_in), (q_hbm, q_in), (d_hbm, d_in), (docs_hbm, docs))
        )
    ]
    for load in loads:
        load.start()

    loads[0].wait()
    row = lax.broadcasted_iota(jnp.int32, (TOK_DEV, DEVICES), 0)
    picks = jnp.transpose(jnp.where(row == pack[...], 1.0, 0.0).astype(F32)).astype(BF16)

    def pair_rows(a, b):
        a = a.reshape(N_DP, BLOCKS, HEAD_WIDTH)
        b = b.reshape(N_DP, BLOCKS, HEAD_WIDTH)
        return jnp.concatenate([a, b], axis=1).astype(BF16)

    loads[1].wait()
    loads[2].wait()
    for j in range(KEY_HEADS):
        cols = slice(j * HEAD_WIDTH, (j + 1) * HEAD_WIDTH)
        kvsend[j] = pair_rows(dot_nn(picks, k_in[:, cols]), dot_nn(picks, v_in[:, cols]))
    loads[3].wait()
    loads[4].wait()

    def pack_head(h):
        for c in range(N_CTX):
            cols = pl.ds(pl.multiple_of((c * HEADS + h) * HEAD_WIDTH, HEAD_WIDTH), HEAD_WIDTH)
            send[h, c * N_DP : (c + 1) * N_DP] = pair_rows(dot_nn(picks, q_in[:, cols]), dot_nn(picks, d_in[:, cols]))

    pack_head(0)
    pl.semaphore_wait(barrier, DEVICES - 1)

    def send_kv_to(chip_offset):
        target = shifted(me - core, 2 * chip_offset) + half
        s, c = target // N_CTX, target % N_CTX
        return pltpu.make_async_remote_copy(
            src_ref=kvsend.at[c // 2, s], dst_ref=kvrecv.at[me], send_sem=kvs_sem, recv_sem=kvr_sem,
            device_id={"dp": s, "ctx": c}, device_id_type=MESH,
        )

    def send_kv(i, carry):
        send_kv_to((i * STRIDE) & 63).start()
        return carry

    @pl.when(core == half)
    def _():
        pltpu.make_async_copy(kvsend.at[my_key, my_dp], kvrecv.at[me], kvr_sem).start()

    @pl.when(core != half)
    def _():
        send_kv_to(0).start()

    lax.fori_loop(1, 64, send_kv, 0)

    def send_head(h):
        def step(i, carry):
            target = shifted(me, (i * STRIDE) & 127)
            s, c = target // N_CTX, target % N_CTX
            pltpu.make_async_remote_copy(
                src_ref=send.at[h, c * N_DP + s], dst_ref=recv.at[h, me], send_sem=in_send.at[h], recv_sem=in_recv.at[h],
                device_id={"dp": s, "ctx": c}, device_id_type=MESH,
            ).start()
            return carry

        pltpu.make_async_copy(send.at[h, my_ctx * N_DP + my_dp], recv.at[h, me], in_recv.at[h]).start()
        lax.fori_loop(1, DEVICES, step, 0)

    send_head(0)

    def pack_and_send(h, carry):
        pack_head(h)
        send_head(h)
        return carry

    lax.fori_loop(1, HEADS, pack_and_send, 0)

    loads[5].wait()
    doc_line = docs[...].astype(F32)
    for k in range(BLOCKS):
        block = jnp.broadcast_to(doc_line[:, k * 128 : (k + 1) * 128], (128, 128))
        scr[k * 128 : (k + 1) * 128] = jnp.transpose(block)
    for i, (lo, hi) in enumerate(WINDOWS):
        for t in range(lo, hi, 128):
            key_doc = scr[t : t + 128]
            for n in range(QB // 128):
                q0 = i * QB + n * 128
                query_doc = doc_line[:, q0 : q0 + 128]
                tpos = t + lax.broadcasted_iota(jnp.int32, (128, 128), 0)
                qpos = q0 + lax.broadcasted_iota(jnp.int32, (128, 128), 1)
                live = (key_doc == query_doc) & (tpos <= qpos)
                at_row = BIAS_ROWS[i] + t - lo
                bias[at_row : at_row + 128, n * 128 : (n + 1) * 128] = jnp.where(live, 0.0, -1e30)
    dks[...] = jnp.zeros_like(dks)
    dvs[...] = jnp.zeros_like(dvs)

    wait_bytes(kvrecv.at[pl.ds(0, 64)], kvr_sem)
    mine = kvrecv.at[pl.ds(core * 64, 64)]
    swap = pltpu.make_async_remote_copy(
        src_ref=mine, dst_ref=mine, send_sem=kvx_sem.at[0], recv_sem=kvx_sem.at[1], device_id=sibling, device_id_type=MESH
    )
    swap.start()
    swap.wait()
    scr[...] = kvrecv[...].reshape(2 * SEQ, HEAD_WIDTH).astype(F32)
    for k in range(BLOCKS):
        rows = slice(k * 128, (k + 1) * 128)
        k_block = scr[pl.ds(k, 128, stride=16), :]
        v_block = scr[pl.ds(BLOCKS + k, 128, stride=16), :]
        ks[rows] = k_block.astype(BF16)
        vs[rows] = v_block.astype(BF16)
        kts[:, rows] = jnp.transpose(k_block).astype(BF16)
        vts[:, rows] = jnp.transpose(v_block).astype(BF16)

    def one_head(h, carry):
        wait_bytes(recv.at[h], in_recv.at[h])
        scr[...] = recv[h].reshape(2 * SEQ, HEAD_WIDTH).astype(F32)
        for k in range(BLOCKS):
            rows = slice(k * 128, (k + 1) * 128)
            qs[rows] = scr[pl.ds(k, 128, stride=16), :].astype(BF16)
            d_block = scr[pl.ds(BLOCKS + k, 128, stride=16), :]
            ds[rows] = d_block.astype(BF16)
            dts[:, rows] = jnp.transpose(d_block)
        for i, (lo, hi) in enumerate(WINDOWS):
            q_rows = slice(i * QB, (i + 1) * QB)
            query, cotangent = qs[q_rows], ds[q_rows]
            scores = dot_nt(ks[lo:hi], query) + bias[BIAS_ROWS[i] : BIAS_ROWS[i + 1]]
            best = jnp.max(scores, axis=0, keepdims=True)
            weights = jnp.exp2((scores - best) * (SCALE * math.log2(math.e)))
            total = jnp.sum(weights, axis=0, keepdims=True)
            probs = weights * (1.0 / total)
            probs_b = probs.astype(BF16)
            out_t = dot_nn(vts[:, lo:hi], probs_b)
            delta = jnp.sum(out_t.astype(BF16).astype(F32) * dts[:, q_rows], axis=0, keepdims=True)
            dprob = dot_nt(vs[lo:hi], cotangent)
            dscore = (probs * (dprob - delta) * SCALE).astype(BF16)
            gq_t = dot_nn(kts[:, lo:hi], dscore)
            dks[lo:hi] += dot_nn(dscore, query)
            dvs[lo:hi] += dot_nn(probs_b, cotangent)
            for n in range(QB // 128):
                k = i * (QB // 128) + n
                lanes = slice(n * 128, (n + 1) * 128)
                scr2[pl.ds(k, 128, stride=16), :] = jnp.transpose(out_t[:, lanes])
                scr2[pl.ds(BLOCKS + k, 128, stride=16), :] = jnp.transpose(gq_t[:, lanes])
        outb[h] = scr2[...].astype(BF16).reshape(DEVICES, 16, HEAD_WIDTH)

        def step(n, inner):
            target = shifted(me, (n * STRIDE) & 127)
            pltpu.make_async_remote_copy(
                src_ref=outb.at[h, target], dst_ref=ret.at[h, my_ctx, my_dp], send_sem=out_send.at[h],
                recv_sem=out_recv.at[h], device_id=at(target), device_id_type=MESH,
            ).start()
            return inner

        pltpu.make_async_copy(outb.at[h, me], ret.at[h, my_ctx, my_dp], out_recv.at[h]).start()
        lax.fori_loop(1, DEVICES, step, 0)
        return carry

    lax.fori_loop(0, HEADS, one_head, 0)

    for k in range(BLOCKS):
        rows = slice(k * 128, (k + 1) * 128)
        scr[pl.ds(k, 128, stride=16), :] = dks[rows]
        scr[pl.ds(BLOCKS + k, 128, stride=16), :] = dvs[rows]
    swap_back = pltpu.make_async_remote_copy(
        src_ref=scr.at[pl.ds(pl.multiple_of((1 - core) * SEQ, SEQ), SEQ)], dst_ref=xbuf, send_sem=dx_sem.at[0], recv_sem=dx_sem.at[1],
        device_id=sibling, device_id_type=MESH,
    )
    swap_back.start()
    swap_back.wait()
    own_half = scr[pl.ds(pl.multiple_of(core * SEQ, SEQ), SEQ), :]
    kvout[...] = (own_half + xbuf[...]).astype(BF16).reshape(64, 16, HEAD_WIDTH)

    def return_kv_to(offset):
        slot = shifted(me, offset) & 63
        return pltpu.make_async_remote_copy(
            src_ref=kvout.at[slot], dst_ref=retkv.at[my_key, my_dp], send_sem=ks_sem, recv_sem=kr_sem,
            device_id=at(core * 64 + slot), device_id_type=MESH,
        )

    def return_kv(i, carry):
        return_kv_to((i * STRIDE) & 63).start()
        return carry

    @pl.when(core == half)
    def _():
        pltpu.make_async_copy(kvout.at[me - half * 64], retkv.at[my_key, my_dp], kr_sem).start()

    @pl.when(core != half)
    def _():
        return_kv_to(0).start()

    lax.fori_loop(1, 64, return_kv, 0)

    for h in range(HEADS):
        wait_bytes(ret.at[h], out_recv.at[h])
    wait_bytes(retkv, kr_sem)
    for h in range(HEADS):
        wait_bytes(send.at[h, pl.ds(0, DEVICES - 1)], in_send.at[h])
        wait_bytes(outb.at[h, pl.ds(0, DEVICES - 1)], out_send.at[h])

    @pl.when(core == half)
    def _():
        wait_bytes(kvrecv.at[pl.ds(0, 63)], kvs_sem)
        wait_bytes(kvout.at[pl.ds(0, 63)], ks_sem)

    @pl.when(core != half)
    def _():
        wait_bytes(kvrecv.at[pl.ds(0, 64)], kvs_sem)
        wait_bytes(kvout.at[pl.ds(0, 64)], ks_sem)


def unpack_kernel(pack, ret, retkv, out, gq, gk, gv):
    row = lax.broadcasted_iota(jnp.int32, (TOK_DEV, DEVICES), 0)
    picks = jnp.where(row == pack[...], 1.0, 0.0).astype(BF16)
    device = lax.broadcasted_iota(jnp.int32, (DEVICES, 2 * DEVICES), 0)
    lane = lax.broadcasted_iota(jnp.int32, (DEVICES, 2 * DEVICES), 1)
    same = device == (lane >> 4) * BLOCKS + (lane & 7)
    upper = ((lane >> 3) & 1) == 1
    spread = [jnp.where(same & (upper == bool(t)), 1.0, 0.0).astype(BF16) for t in range(2)]
    place = jnp.concatenate([dot_nn(picks, e) for e in spread], axis=0).astype(BF16)

    for h in range(HEADS):
        cols = slice(h * HEAD_WIDTH, (h + 1) * HEAD_WIDTH)
        both = dot_nn(place, ret[h, 0].reshape(2 * DEVICES, HEAD_WIDTH))
        out[:, cols] = both[:TOK_DEV].astype(BF16)
        gq[:, cols] = both[TOK_DEV:]

    @pl.when(pl.program_id(0) == 0)
    def _():
        for j in range(KEY_HEADS):
            cols = slice(j * HEAD_WIDTH, (j + 1) * HEAD_WIDTH)
            both = dot_nn(place, retkv[j].reshape(2 * DEVICES, HEAD_WIDTH))
            gk[:, cols] = both[:TOK_DEV]
            gv[:, cols] = both[TOK_DEV:]


def local(queries, loader_key_rows, loader_value_rows, output_gradient, packing, documents):
    slots = (DEVICES, 16, HEAD_WIDTH)
    ret, retkv = pl.pallas_call(
        main_kernel,
        out_shape=(
            jax.ShapeDtypeStruct((HEADS, N_CTX, N_DP, 16, HEAD_WIDTH), BF16),
            jax.ShapeDtypeStruct((KEY_HEADS, N_DP, 16, HEAD_WIDTH), BF16),
        ),
        in_specs=[pl.BlockSpec(memory_space=pl.ANY)] * 6,
        out_specs=(pl.BlockSpec(memory_space=pl.ANY),) * 2,
        scratch_shapes=[
            pltpu.VMEM(queries.shape, BF16),
            pltpu.VMEM(loader_key_rows.shape, BF16),
            pltpu.VMEM(loader_value_rows.shape, BF16),
            pltpu.VMEM(output_gradient.shape, BF16),
            pltpu.VMEM(packing.shape, jnp.int32),
            pltpu.VMEM(documents.shape, jnp.int32),
            pltpu.VMEM((HEADS, *slots), BF16),
            pltpu.VMEM((HEADS, *slots), BF16),
            pltpu.VMEM((HEADS, *slots), BF16),
            pltpu.VMEM((KEY_HEADS, N_DP, 16, HEAD_WIDTH), BF16),
            pltpu.VMEM(slots, BF16),
            pltpu.VMEM((64, 16, HEAD_WIDTH), BF16),
            pltpu.VMEM((SEQ, HEAD_WIDTH), F32),
            pltpu.VMEM((2 * SEQ, HEAD_WIDTH), F32),
            pltpu.VMEM((2 * SEQ, HEAD_WIDTH), F32),
            pltpu.VMEM((SEQ, HEAD_WIDTH), BF16),
            pltpu.VMEM((SEQ, HEAD_WIDTH), BF16),
            pltpu.VMEM((HEAD_WIDTH, SEQ), F32),
            pltpu.VMEM((SEQ, HEAD_WIDTH), BF16),
            pltpu.VMEM((SEQ, HEAD_WIDTH), BF16),
            pltpu.VMEM((HEAD_WIDTH, SEQ), BF16),
            pltpu.VMEM((HEAD_WIDTH, SEQ), BF16),
            pltpu.VMEM((SEQ, HEAD_WIDTH), F32),
            pltpu.VMEM((SEQ, HEAD_WIDTH), F32),
            pltpu.VMEM((BIAS_ROWS[-1], QB), F32),
            pltpu.SemaphoreType.DMA((6,)),
            pltpu.SemaphoreType.DMA((HEADS,)),
            pltpu.SemaphoreType.DMA((HEADS,)),
            pltpu.SemaphoreType.DMA((HEADS,)),
            pltpu.SemaphoreType.DMA((HEADS,)),
            pltpu.SemaphoreType.DMA,
            pltpu.SemaphoreType.DMA,
            pltpu.SemaphoreType.DMA((2,)),
            pltpu.SemaphoreType.DMA,
            pltpu.SemaphoreType.DMA,
            pltpu.SemaphoreType.DMA((2,)),
        ],
        compiler_params=pltpu.CompilerParams(collective_id=0, has_side_effects=True, vmem_limit_bytes=48 << 20),
        name="exchange_attention",
    )(queries, loader_key_rows, loader_value_rows, output_gradient, packing, documents)

    wide = HEADS * HEAD_WIDTH
    kv_shape = (TOK_DEV, KEY_HEADS * HEAD_WIDTH)
    return pl.pallas_call(
        unpack_kernel,
        grid=(N_CTX,),
        out_shape=(
            jax.ShapeDtypeStruct(queries.shape, BF16),
            jax.ShapeDtypeStruct(queries.shape, F32),
            jax.ShapeDtypeStruct(kv_shape, F32),
            jax.ShapeDtypeStruct(kv_shape, F32),
        ),
        in_specs=[
            pl.BlockSpec((1, TOK_DEV), lambda c: (0, 0)),
            pl.BlockSpec((HEADS, 1, N_DP, 16, HEAD_WIDTH), lambda c: (0, c, 0, 0, 0)),
            pl.BlockSpec((KEY_HEADS, N_DP, 16, HEAD_WIDTH), lambda c: (0, 0, 0, 0)),
        ],
        out_specs=(
            pl.BlockSpec((TOK_DEV, wide), lambda c: (0, c)),
            pl.BlockSpec((TOK_DEV, wide), lambda c: (0, c)),
            pl.BlockSpec(kv_shape, lambda c: (0, 0)),
            pl.BlockSpec(kv_shape, lambda c: (0, 0)),
        ),
        name="rows_to_loader_order",
    )(packing, ret, retkv)


def solution(mesh):
    rows = P(("dp", "ctx"), None)
    return jax.shard_map(
        local, mesh=mesh, in_specs=(rows,) * 5 + (P("dp", None),), out_specs=(rows,) * 4, check_vma=False
    )
```

time: 487 us -> 82.1 us (0.17); the launches traced: 479 us -> 81.7 us
  local copies, waits for them, and re-layouts: 134 us -> 7.63 us
  waiting for transfers between devices: 115 us -> 0 us
  starting transfers between devices: 104 us -> 0 us
  Pallas kernels: 0 us -> 73.4 us
  other arithmetic: 50.5 us -> 0 us
  loops' own time: 35 us -> 0 us
  matrix products: 25.5 us -> 0 us
  between operations: 14.6 us -> 0.66 us
    all_to_all x8 -> x0, waiting for transfers between devices: 115 us -> none  [the longest x1 36.6 us: local(): lax.all_to_all(out_rows, ('dp', 'ctx'), split_axis=0, concat_axis=0, tile...]
    all_to_all x8 -> x0, starting transfers between devices: 103 us -> none  [the longest x1 61.3 us: local(): lax.all_to_all(grad_query_rows, ('dp', 'ctx'), split_axis=0, concat_axis=...]
    pallas_call x0 -> x2, Pallas kernels: none -> 73.4 us  [the longest x1 65.5 us: local(): pl.pallas_call(main_kernel, out_shape=(jax.ShapeDtypeStruct((HEADS, N_CTX...]
    gather x54 -> x0, local copies, waits for them, and re-layouts: 54.2 us -> none  [the longest x48 46.6 us: shard_mask(): key_doc = jnp.take(doc_line, key_pos)]
    another operation x54 -> x0, loops' own time: 35 us -> none  [the longest x2 11.4 us: local(): lax.fori_loop(0, context_count, backward_step, (initial_gradient, key_gra...]
    reduce_or x48 -> x0, other arithmetic: 34.5 us -> none  [the longest x16 11.5 us: output_update(): return lax.cond(jnp.any(causal_mask), live_output, keep_carry, carry)]
    dot_general x28 -> x0, matrix products: 25.5 us -> none  [the longest x4 8.09 us: live_backward(): jnp.einsum('grqk,qgrd->kgd', probs_b, grad_half, preferred_element_type=j...]
    unnamed x46 -> x16, local copies, waits for them, and re-layouts: 22.4 us -> 7.63 us
  transfers between devices with their start and end apart: 12 -> 0, of which waited for: 7 -> 0; matrix products, arithmetic and copies ran while one was open for 17% -> 0% of each run, Pallas kernels for 0% -> 0%
where the time goes in v1:
time: 82.1 us; the launch traced here: 81.7 us
  Pallas kernels  73.4 us (89%)
  local copies, waits for them, and re-layouts  7.63 us (9%)
    pallas_call x1, Pallas kernels, local(): pl.pallas_call(main_kernel, out_shape=(jax.ShapeDtypeStruct((HEADS, N_CTX...  65.5 us
    pallas_call x1, Pallas kernels, local(): pl.pallas_call(unpack_kernel, grid=(N_CTX,), out_shape=(jax.ShapeDtypeStr...  7.84 us
    unnamed x16, local copies, waits for them, and re-layouts  7.63 us

profile of v1, /device:TPU:1, one launch (start us, length us, event | category | flops | bytes accessed | tf_op | source)
XLA Modules:
  0.0 81.7 jit_solution(12231419586080248898)
XLA Ops:
  0.6 0.0 copy-start.1
  0.6 1.2 %copy-done.1 = bf16[128,4096]{1,0:T(8,128)(2,1)S(1)} copy-done((bf16[128,4096]{1,0:T(8,128)(2,1)S(1)}, bf16[128,4096]{1,0:T(8,128)(2,1)}, u32[]{:S(2)}) %copy-start.1) | copy-done | bytes 1048600
  1.9 0.0 copy-start.2
  1.9 1.2 %copy-done.2 = bf16[128,4096]{1,0:T(8,128)(2,1)S(1)} copy-done((bf16[128,4096]{1,0:T(8,128)(2,1)S(1)}, bf16[128,4096]{1,0:T(8,128)(2,1)}, u32[]{:S(2)}) %copy-start.2) | copy-done | bytes 1048600
  3.1 0.0 copy-start.4
  3.1 0.9 %copy-done.4 = bf16[128,512]{1,0:T(8,128)(2,1)S(1)} copy-done((bf16[128,512]{1,0:T(8,128)(2,1)S(1)}, bf16[128,512]{1,0:T(8,128)(2,1)}, u32[]{:S(2)}) %copy-start.4) | copy-done | bytes 131096
  4.0 0.0 copy-start.5
  4.0 0.9 %copy-done.5 = bf16[128,512]{1,0:T(8,128)(2,1)S(1)} copy-done((bf16[128,512]{1,0:T(8,128)(2,1)S(1)}, bf16[128,512]{1,0:T(8,128)(2,1)}, u32[]{:S(2)}) %copy-start.5) | copy-done | bytes 131096
  4.9 0.0 copy-start.6
  4.9 0.7 copy-done.6
  5.6 0.0 copy-start.7
  5.6 0.7 copy-done.7
  6.2 65.5 %exchange_attention.1 = (bf16[4,8,16,16,128]{4,3,2,1,0:T(8,128)(2,1)S(1)}, bf16[4,16,16,128]{3,2,1,0:T(8,128)(2,1)S(1)}) custom-call(bf16[128,4096]{1,0:T(8,128)(2,1)S(1)} %copy-done.1, bf16[128,512]{1,0:T(8,128)(2,1)S(1)} %copy-done.4, bf16[128,512]{1,0:T(8,128)(2,1)S(1)} %copy-done.5, bf16[128,4096]{1,0:T(8,128)(2,1)S(1)} %copy-done.2, ...), custom_call_target="tpu_custom_call" | custom-call | tf_op jit(solution)/shard_map/exchange_attention/pallas_call | solution.py:315
  71.8 0.0 copy-start
  71.8 1.3 %copy-done = bf16[4,8,16,16,128]{4,3,2,1,0:T(8,128)(2,1)} copy-done((bf16[4,8,16,16,128]{4,3,2,1,0:T(8,128)(2,1)}, bf16[4,8,16,16,128]{4,3,2,1,0:T(8,128)(2,1)S(1)}, u32[]{:S(2)}) %copy-start) | copy-done | bytes 2097176
  73.1 0.0 copy-start.3
  73.1 0.7 copy-done.3
  73.8 7.8 %rows_to_loader_order.1 = (bf16[128,4096]{1,0:T(8,128)(2,1)}, f32[128,4096]{1,0:T(8,128)}, f32[128,512]{1,0:T(8,128)}, f32[128,512]{1,0:T(8,128)}) custom-call(s32[1,128]{1,0:T(1,128)} %pack.1, bf16[4,8,16,16,128]{4,3,2,1,0:T(8,128)(2,1)} %copy-done, bf16[4,16,16,128]{3,2,1,0:T(8,128)(2,1)} %copy-done.3), custom_call_target="tpu_custom_call" | custom-call | tf_op jit(solution)/shard_map/rows_to_loader_order/pallas_call | solution.py:367
Async XLA Ops:
  0.6 1.2 %copy-start.1 = (bf16[128,4096]{1,0:T(8,128)(2,1)S(1)}, bf16[128,4096]{1,0:T(8,128)(2,1)}, u32[]{:S(2)}) copy-start(bf16[128,4096]{1,0:T(8,128)(2,1)} %q_hbm.1) | copy-start | bytes 3145732
  1.9 1.2 %copy-start.2 = (bf16[128,4096]{1,0:T(8,128)(2,1)S(1)}, bf16[128,4096]{1,0:T(8,128)(2,1)}, u32[]{:S(2)}) copy-start(bf16[128,4096]{1,0:T(8,128)(2,1)} %d_hbm.1) | copy-start | bytes 3145732
  3.1 0.9 %copy-start.4 = (bf16[128,512]{1,0:T(8,128)(2,1)S(1)}, bf16[128,512]{1,0:T(8,128)(2,1)}, u32[]{:S(2)}) copy-start(bf16[128,512]{1,0:T(8,128)(2,1)} %k_hbm.1) | copy-start | bytes 393220
  4.0 0.9 %copy-start.5 = (bf16[128,512]{1,0:T(8,128)(2,1)S(1)}, bf16[128,512]{1,0:T(8,128)(2,1)}, u32[]{:S(2)}) copy-start(bf16[128,512]{1,0:T(8,128)(2,1)} %v_hbm.1) | copy-start | bytes 393220
  4.9 0.7 copy-start.6
  5.6 0.7 copy-start.7
  71.8 1.3 %copy-start = (bf16[4,8,16,16,128]{4,3,2,1,0:T(8,128)(2,1)}, bf16[4,8,16,16,128]{4,3,2,1,0:T(8,128)(2,1)S(1)}, u32[]{:S(2)}) copy-start(bf16[4,8,16,16,128]{4,3,2,1,0:T(8,128)(2,1)S(1)} %get-tuple-element.6.ret) | copy-start | bytes 6291460
  73.1 0.7 copy-start.3

commit v2 on v1

v2 whole, which is shorter than its diff:
```python
import math

import jax
import jax.numpy as jnp
from jax import lax
from jax.experimental import pallas as pl
from jax.experimental.pallas import tpu as pltpu
from jax.sharding import PartitionSpec as P

HEAD_WIDTH = 128
TOK_DEV = 128
N_CTX = 8
DEVICES = 128
SEQUENCES = 16
KEY_HEADS = 4
BLOCKS = 8
SEQ = 1024
QB = 256
DOC_MOST = 512
SCALE = 1.0 / math.sqrt(HEAD_WIDTH)
MESH = pl.DeviceIdType.MESH
F32 = jnp.float32
BF16 = jnp.bfloat16

Z, Y, X = range(3)
UNITS = KEY_HEADS
OWN = 2
CHUNKS = 2
CHUNK_HEADS = 4
PLANE = 32
ROWS = CHUNK_HEADS * 16
STRIDE = 13

WINDOWS = [(max(0, QB * i - DOC_MOST), QB * (i + 1)) for i in range(SEQ // QB)]
BIAS_ROWS = [sum(b - a for a, b in WINDOWS[:i]) for i in range(len(WINDOWS) + 1)]


def shifted(index, offset):
    low = 0b01010
    return (((index & low) + (offset & low)) ^ ((index ^ offset) & (31 - low))) & 31


def dot_nt(a, b):
    return lax.dot_general(a, b, (((1,), (1,)), ((), ())), preferred_element_type=F32)


def dot_nn(a, b):
    return jnp.dot(a, b, preferred_element_type=F32)


def wait_bytes(ref, sem):
    pltpu.make_async_copy(ref, ref, sem).wait()


def main_kernel(
    q_hbm, k_hbm, v_hbm, d_hbm, pack_hbm, docs_hbm,
    ret, retkv, place,
    q_in, k_in, v_in, d_in, pack, docs,
    send, recv, outb, kvsend, kv, kvout, dkv, pxs, pxr,
    scr, scr2, ks, vs, kts, vts, dks, dvs, bias,
    load_sem, in_send, in_recv, out_send, out_recv, doc_send, doc_recv,
    kvs_sem, kvr_sem, ks_sem, kr_sem, fws_sem, fwr_sem, pxs_sem, pxr_sem,
):
    my_dp = lax.axis_index("dp")
    my_ctx = lax.axis_index("ctx")
    z, y, x, core = my_dp // 4, my_dp % 4, my_ctx // 2, my_ctx % 2
    first = {Z: y, Y: z, X: z}
    second = {Z: x, Y: x, X: y}
    plane = {Z: z, Y: y, X: x}
    mine = {kind: first[kind] * 8 + second[kind] * 2 + core for kind in (Z, Y, X)}
    kinds = [u % 3 for u in range(UNITS)]

    def device(kind, index):
        a, b, c = index // 8, (index // 2) % 4, index % 2
        if kind == Z:
            return {"dp": z * 4 + a, "ctx": b * 2 + c}
        if kind == Y:
            return {"dp": a * 4 + y, "ctx": b * 2 + c}
        return {"dp": a * 4 + b, "ctx": x * 2 + c}

    def sequence(kind, index):
        a, b = index // 8, (index // 2) % 4
        return b * 4 + a if kind == Z else a * 4 + b

    def peer(kind, p):
        if kind == Z:
            return {"dp": p * 4 + y, "ctx": my_ctx}
        if kind == Y:
            return {"dp": z * 4 + p, "ctx": my_ctx}
        return {"dp": my_dp, "ctx": p * 2 + core}

    def remote(src, dst, send_sem, recv_sem, to):
        return pltpu.make_async_remote_copy(
            src_ref=src, dst_ref=dst, send_sem=send_sem, recv_sem=recv_sem, device_id=to, device_id_type=MESH
        )

    def loaders_of(ref, kind, p):
        every = slice(None)
        return ref.at[{Z: (p,), Y: (every, p), X: (every, every, p)}[kind]]

    def for_own(w, body):
        for c in range(2):
            u = c * OWN + w
            pl.when(core == c)(lambda u=u: body(u, kinds[u]))

    def to_chips(units, copy_to, own_copy):
        units = [(u, kinds[u]) for u in units]

        def step(i, carry):
            for u, kind in units:
                copy_to(u, kind, shifted(mine[kind] - core, 2 * ((i * STRIDE) & 15)) + u // OWN).start()
            return carry

        for u, kind in units:
            pl.when(core == u // OWN)(lambda u=u, kind=kind: own_copy(u, kind).start())
            pl.when(core != u // OWN)(lambda u=u, kind=kind: copy_to(u, kind, mine[kind] - core + u // OWN).start())
        lax.fori_loop(1, 16, step, 0)

    barrier = pltpu.get_barrier_semaphore()

    def greet(i, carry):
        for kind in (Z, Y, X):
            to = device(kind, shifted(mine[kind], (i * STRIDE) & 31))
            pl.semaphore_signal(barrier, inc=1, device_id=to, device_id_type=MESH)
        return carry

    lax.fori_loop(1, PLANE, greet, 0)

    load_kv = [
        pltpu.make_async_copy(src, dst, load_sem.at[i])
        for i, (src, dst) in enumerate(((pack_hbm, pack), (k_hbm, k_in), (v_hbm, v_in), (docs_hbm, docs.at[X])))
    ]
    for load in load_kv:
        load.start()
    part_wide = CHUNK_HEADS * HEAD_WIDTH
    for ch in range(CHUNKS):
        for u in range(UNITS):
            cols = pl.ds((u * CHUNKS + ch) * part_wide, part_wide)
            pltpu.make_async_copy(q_hbm.at[:, cols], q_in.at[:, cols], load_sem.at[4 + 2 * ch]).start()
            pltpu.make_async_copy(d_hbm.at[:, cols], d_in.at[:, cols], load_sem.at[5 + 2 * ch]).start()

    load_kv[0].wait()
    row = lax.broadcasted_iota(jnp.int32, (TOK_DEV, DEVICES), 0)
    by_row = jnp.where(row == pack[...], 1.0, 0.0).astype(F32)
    picks = jnp.transpose(by_row).astype(BF16)

    def pair_rows(a, b):
        a = a.reshape(SEQUENCES, BLOCKS, HEAD_WIDTH)
        b = b.reshape(SEQUENCES, BLOCKS, HEAD_WIDTH)
        return jnp.concatenate([a, b], axis=1).astype(BF16)

    load_kv[1].wait()
    load_kv[2].wait()
    for u in range(UNITS):
        cols = slice(u * HEAD_WIDTH, (u + 1) * HEAD_WIDTH)
        kvsend[u] = pair_rows(dot_nn(picks, k_in[:, cols]), dot_nn(picks, v_in[:, cols]))

    def pack_chunk(ch):
        wait_bytes(q_in.at[:, pl.ds(0, UNITS * part_wide)], load_sem.at[4 + 2 * ch])
        wait_bytes(d_in.at[:, pl.ds(0, UNITS * part_wide)], load_sem.at[5 + 2 * ch])
        for u in range(UNITS):
            for h in range(CHUNK_HEADS):
                head = (u * CHUNKS + ch) * CHUNK_HEADS + h
                cols = slice(head * HEAD_WIDTH, (head + 1) * HEAD_WIDTH)
                tile = pair_rows(dot_nn(picks, q_in[:, cols]), dot_nn(picks, d_in[:, cols]))
                send[ch, u, :, h * 16 : (h + 1) * 16] = tile

    pack_chunk(0)
    pl.semaphore_wait(barrier, 3 * (PLANE - 1))

    to_chips(
        range(UNITS),
        lambda u, kind, n: remote(
            kvsend.at[u, sequence(kind, n)], kv.at[u % OWN, plane[kind], mine[kind]],
            kvs_sem.at[u], kvr_sem.at[u % OWN], device(kind, n),
        ),
        lambda u, kind: pltpu.make_async_copy(
            kvsend.at[u, sequence(kind, mine[kind])], kv.at[u % OWN, plane[kind], mine[kind]], kvr_sem.at[u % OWN]
        ),
    )

    load_kv[3].wait()
    doc_to = {Z: {"dp": x * 4 + y, "ctx": z * 2 + core}, Y: {"dp": z * 4 + x, "ctx": y * 2 + core}}
    doc_stays = {Z: x == z, Y: x == y}
    for kind in (Z, Y):

        @pl.when(doc_stays[kind])
        def _():
            pltpu.make_async_copy(docs.at[X], docs.at[kind], doc_recv.at[kind]).start()

        @pl.when(jnp.logical_not(doc_stays[kind]))
        def _():
            remote(docs.at[X], docs.at[kind], doc_send.at[kind], doc_recv.at[kind], doc_to[kind]).start()

    def send_chunk(ch, w):
        to_chips(
            range(w, UNITS, OWN),
            lambda u, kind, n: remote(
                send.at[ch, u, sequence(kind, n)], recv.at[ch, u % OWN, mine[kind]],
                in_send.at[ch, u], in_recv.at[ch, u % OWN], device(kind, n),
            ),
            lambda u, kind: pltpu.make_async_copy(
                send.at[ch, u, sequence(kind, mine[kind])], recv.at[ch, u % OWN, mine[kind]], in_recv.at[ch, u % OWN]
            ),
        )

    def hand_on(u, kind):
        block = kv.at[u % OWN, plane[kind]]
        for d in range(1, 4):
            to = peer(kind, (plane[kind] + d) % 4)
            remote(block, block, fws_sem.at[u % OWN], fwr_sem.at[u % OWN], to).start()

    send_chunk(0, 0)
    pack_chunk(1)
    for w in range(OWN):
        wait_bytes(kv.at[w, 0], kvr_sem.at[w])
        for_own(w, hand_on)
    send_chunk(0, 1)
    send_chunk(1, 0)
    send_chunk(1, 1)

    goes = lax.broadcasted_iota(jnp.int32, (DEVICES, 2 * DEVICES), 0)
    lane = lax.broadcasted_iota(jnp.int32, (DEVICES, 2 * DEVICES), 1)
    same = goes == (lane >> 4) * BLOCKS + (lane & 7)
    upper = ((lane >> 3) & 1) == 1
    for t in range(2):
        spread = jnp.where(same & (upper == bool(t)), 1.0, 0.0).astype(BF16)
        place[t * TOK_DEV : (t + 1) * TOK_DEV] = dot_nn(by_row.astype(BF16), spread).astype(BF16)
    dks[...] = jnp.zeros_like(dks)
    dvs[...] = jnp.zeros_like(dvs)

    tile = (128, 128)
    lanes = lax.broadcasted_iota(jnp.int32, tile, 1)
    sub = lax.broadcasted_iota(jnp.int32, tile, 0)
    m = lanes >> 2
    loader = {Z: z * 32 + m, Y: (m >> 3) * 32 + y * 8 + (m & 7), X: (m >> 1) * 8 + x * 2 + (m & 1)}
    flat = scr.reshape(2 * SEQ, HEAD_WIDTH)
    for kind in (Y, Z):
        wait_bytes(docs.at[kind], doc_recv.at[kind])
    for w in range(OWN):
        query_at = jnp.where(core == 0, loader[kinds[w]], loader[kinds[OWN + w]])
        line = docs[jnp.where(core == 0, kinds[w], kinds[OWN + w])].astype(F32)
        parts = [line[:, k * 128 : (k + 1) * 128] for k in range(BLOCKS)]
        for k in range(BLOCKS):
            flat[k * 128 : (k + 1) * 128] = jnp.transpose(jnp.broadcast_to(parts[k], tile))
        select = jnp.where(sub == query_at, 1.0, 0.0).astype(BF16)
        query_docs = dot_nn(jnp.concatenate(parts, axis=0).astype(BF16), select)
        for i, (lo, hi) in enumerate(WINDOWS):
            for t in range(lo, hi, 128):
                for n in range(2):
                    k = 2 * i + n
                    live = (flat[t : t + 128] == query_docs[k : k + 1]) & (t + sub <= k * 128 + query_at)
                    at_row = BIAS_ROWS[i] + t - lo
                    bias[w, at_row : at_row + 128, n * 128 : (n + 1) * 128] = jnp.where(live, 0.0, -1e30)

    def keys_in_order(w):
        wait_bytes(kv.at[w, pl.ds(0, 3)], fwr_sem.at[w])

        def spread_kv(u, kind):
            for p in range(4):
                part = loaders_of(scr, kind, p)
                part[...] = kv[w, p].reshape(part.shape).astype(F32)

        for_own(w, spread_kv)
        for k in range(BLOCKS):
            rows = slice(k * 128, (k + 1) * 128)
            k_block = flat[pl.ds(k, 128, stride=16), :]
            v_block = flat[pl.ds(BLOCKS + k, 128, stride=16), :]
            ks[w, rows] = k_block.astype(BF16)
            vs[w, rows] = v_block.astype(BF16)
            kts[w, :, rows] = jnp.transpose(k_block).astype(BF16)
            vts[w, :, rows] = jnp.transpose(v_block).astype(BF16)

    def one_step(n, carry):
        ch, w = n // OWN, n % OWN
        for own in range(OWN):
            pl.when(n == own)(lambda own=own: keys_in_order(own))
        wait_bytes(recv.at[ch, w], in_recv.at[ch, w])
        flat[...] = recv[ch, w].reshape(2 * SEQ, HEAD_WIDTH).astype(F32)
        for i, (lo, hi) in enumerate(WINDOWS):

            def pair(start):
                parts = [flat[pl.ds(start + 2 * i + n, 128, stride=16), :] for n in range(2)]
                return jnp.concatenate(parts, axis=0)

            query = pair(0).astype(BF16)
            cotangent_f = pair(BLOCKS)
            cotangent = cotangent_f.astype(BF16)
            scores = dot_nt(ks[w, lo:hi], query) + bias[w, BIAS_ROWS[i] : BIAS_ROWS[i + 1]]
            best = jnp.max(scores, axis=0, keepdims=True)
            weights = jnp.exp2((scores - best) * (SCALE * math.log2(math.e)))
            total = jnp.sum(weights, axis=0, keepdims=True)
            probs = weights * (1.0 / total)
            probs_b = probs.astype(BF16)
            out_t = dot_nn(vts[w, :, lo:hi], probs_b)
            delta = jnp.sum(out_t.astype(BF16).astype(F32) * jnp.transpose(cotangent_f), axis=0, keepdims=True)
            dprob = dot_nt(vs[w, lo:hi], cotangent)
            dscore = (probs * (dprob - delta) * SCALE).astype(BF16)
            gq_t = dot_nn(kts[w, :, lo:hi], dscore)
            dks[w, lo:hi] += dot_nn(dscore, query)
            dvs[w, lo:hi] += dot_nn(probs_b, cotangent)
            out_rows, gq_rows = jnp.transpose(out_t), jnp.transpose(gq_t)
            for n in range(2):
                scr2[pl.ds(2 * i + n, 128, stride=16), :] = out_rows[n * 128 : (n + 1) * 128]
                scr2[pl.ds(BLOCKS + 2 * i + n, 128, stride=16), :] = gq_rows[n * 128 : (n + 1) * 128]
        outb[ch, w] = scr2[...].astype(BF16).reshape(PLANE, ROWS, HEAD_WIDTH)

        def exchange_gradients(u, kind):
            for p in range(4):
                dkv[w, p] = loaders_of(scr, kind, p)[...].reshape(PLANE, 16, HEAD_WIDTH)
            pxs[w] = dkv[w].astype(BF16)
            for d in range(1, 4):
                p = (plane[kind] + d) % 4
                remote(pxs.at[w, p], pxr.at[w, plane[kind]], pxs_sem.at[w], pxr_sem.at[w], peer(kind, p)).start()

        @pl.when(ch == CHUNKS - 1)
        def _():
            for k in range(BLOCKS):
                rows = slice(k * 128, (k + 1) * 128)
                flat[pl.ds(k, 128, stride=16), :] = dks[w, rows]
                flat[pl.ds(BLOCKS + k, 128, stride=16), :] = dvs[w, rows]
            for own in range(OWN):
                pl.when(w == own)(lambda own=own: for_own(own, exchange_gradients))

        def return_rows(u, kind):
            slot = ret.at[ch, u, sequence(kind, mine[kind])]

            def step(i, inner):
                to = shifted(mine[kind], (i * STRIDE) & 31)
                remote(outb.at[ch, w, to], slot, out_send.at[ch, w], out_recv.at[ch, u], device(kind, to)).start()
                return inner

            pltpu.make_async_copy(outb.at[ch, w, mine[kind]], slot, out_recv.at[ch, u]).start()
            lax.fori_loop(1, PLANE, step, 0)

        for own in range(OWN):
            pl.when(w == own)(lambda own=own: for_own(own, return_rows))
        return carry

    lax.fori_loop(0, CHUNKS * OWN, one_step, 0)

    def return_kv(u, kind):
        w = u % OWN
        total = dkv[w, plane[kind]]
        for d in range(1, 4):
            total = total + pxr[w, (plane[kind] + d) % 4].astype(F32)
        kvout[w] = total.astype(BF16)
        slot = retkv.at[u, sequence(kind, mine[kind])]

        def step(i, carry):
            to = shifted(mine[kind], (i * STRIDE) & 31)
            remote(kvout.at[w, to], slot, ks_sem.at[w], kr_sem.at[u], device(kind, to)).start()
            return carry

        pltpu.make_async_copy(kvout.at[w, mine[kind]], slot, kr_sem.at[u]).start()
        lax.fori_loop(1, PLANE, step, 0)

    for w in range(OWN):
        wait_bytes(pxr.at[w, pl.ds(0, 3)], pxr_sem.at[w])
        for_own(w, return_kv)

    for u in range(UNITS):
        for ch in range(CHUNKS):
            wait_bytes(ret.at[ch, u], out_recv.at[ch, u])
            wait_bytes(send.at[ch, u, pl.ds(0, 15)], in_send.at[ch, u])
        wait_bytes(retkv.at[u], kr_sem.at[u])
        wait_bytes(kvsend.at[u, pl.ds(0, 15)], kvs_sem.at[u])

        @pl.when(core != u // OWN)
        def _():
            for ch in range(CHUNKS):
                wait_bytes(send.at[ch, u, 0], in_send.at[ch, u])
            wait_bytes(kvsend.at[u, 0], kvs_sem.at[u])

    for w in range(OWN):
        for ch in range(CHUNKS):
            wait_bytes(outb.at[ch, w, pl.ds(0, PLANE - 1)], out_send.at[ch, w])
        wait_bytes(kv.at[w, pl.ds(0, 3)], fws_sem.at[w])
        wait_bytes(pxs.at[w, pl.ds(0, 3)], pxs_sem.at[w])
        wait_bytes(kvout.at[w, pl.ds(0, PLANE - 1)], ks_sem.at[w])
    for kind in (Z, Y):

        @pl.when(jnp.logical_not(doc_stays[kind]))
        def _():
            wait_bytes(docs.at[kind], doc_send.at[kind])


def unpack_kernel(ret, retkv, place, out, gq, gk, gv, out_s, gq_s, gk_s, gv_s, sems):
    copies = []

    def put(src, dst, cols):
        copies.append(pltpu.make_async_copy(src.at[:, cols], dst.at[:, cols], sems.at[len(copies)]))
        copies[-1].start()

    head = 0
    for u in range(UNITS):
        for ch in range(CHUNKS):
            for h in range(CHUNK_HEADS):
                rows = ret[ch, u, :, h * 16 : (h + 1) * 16].reshape(2 * DEVICES, HEAD_WIDTH)
                both = dot_nn(place[...], rows)
                cols = slice(head * HEAD_WIDTH, (head + 1) * HEAD_WIDTH)
                out_s[:, cols] = both[:TOK_DEV].astype(BF16)
                gq_s[:, cols] = both[TOK_DEV:]
                head += 1
            wide = CHUNK_HEADS * HEAD_WIDTH
            put(out_s, out, pl.ds((u * CHUNKS + ch) * wide, wide))
            put(gq_s, gq, pl.ds((u * CHUNKS + ch) * wide, wide))
    for u in range(UNITS):
        cols = slice(u * HEAD_WIDTH, (u + 1) * HEAD_WIDTH)
        both = dot_nn(place[...], retkv[u].reshape(2 * DEVICES, HEAD_WIDTH))
        gk_s[:, cols] = both[:TOK_DEV]
        gv_s[:, cols] = both[TOK_DEV:]
    put(gk_s, gk, pl.ds(0, KEY_HEADS * HEAD_WIDTH))
    put(gv_s, gv, pl.ds(0, KEY_HEADS * HEAD_WIDTH))
    for copy in copies:
        copy.wait()


def local(queries, loader_key_rows, loader_value_rows, output_gradient, packing, documents):
    out_rows = pltpu.VMEM((CHUNKS, UNITS, SEQUENCES, ROWS, HEAD_WIDTH), BF16)
    own_rows = pltpu.VMEM((CHUNKS, OWN, PLANE, ROWS, HEAD_WIDTH), BF16)
    seq = (OWN, SEQ, HEAD_WIDTH)
    turned = (OWN, HEAD_WIDTH, SEQ)
    kv_tiles = (UNITS, SEQUENCES, 16, HEAD_WIDTH)
    planes = (OWN, 4, PLANE, 16, HEAD_WIDTH)

    def copies(*shape):
        return pltpu.SemaphoreType.DMA(shape)

    operands = (queries, loader_key_rows, loader_value_rows, output_gradient, packing, documents)
    operands = [pltpu.with_memory_space_constraint(x, pltpu.HBM) for x in operands]
    ret, retkv, place = pl.pallas_call(
        main_kernel,
        out_shape=(
            jax.ShapeDtypeStruct(out_rows.shape, BF16),
            jax.ShapeDtypeStruct(kv_tiles, BF16),
            jax.ShapeDtypeStruct((2 * TOK_DEV, 2 * DEVICES), BF16),
        ),
        in_specs=[pl.BlockSpec(memory_space=pltpu.HBM)] * 6,
        out_specs=(pl.BlockSpec(memory_space=pltpu.VMEM),) * 3,
        scratch_shapes=[
            pltpu.VMEM(queries.shape, BF16),
            pltpu.VMEM(loader_key_rows.shape, BF16),
            pltpu.VMEM(loader_value_rows.shape, BF16),
            pltpu.VMEM(output_gradient.shape, BF16),
            pltpu.VMEM(packing.shape, jnp.int32),
            pltpu.VMEM((3, *documents.shape), jnp.int32),
            out_rows,
            own_rows,
            own_rows,
            pltpu.VMEM(kv_tiles, BF16),
            pltpu.VMEM(planes, BF16),
            pltpu.VMEM((OWN, PLANE, 16, HEAD_WIDTH), BF16),
            pltpu.VMEM(planes, F32),
            pltpu.VMEM(planes, BF16),
            pltpu.VMEM(planes, BF16),
            pltpu.VMEM((4, 4, 4, 2, 16, HEAD_WIDTH), F32),
            pltpu.VMEM((2 * SEQ, HEAD_WIDTH), F32),
            pltpu.VMEM(seq, BF16),
            pltpu.VMEM(seq, BF16),
            pltpu.VMEM(turned, BF16),
            pltpu.VMEM(turned, BF16),
            pltpu.VMEM(seq, F32),
            pltpu.VMEM(seq, F32),
            pltpu.VMEM((OWN, BIAS_ROWS[-1], QB), F32),
            copies(8),
            copies(CHUNKS, UNITS), copies(CHUNKS, OWN),
            copies(CHUNKS, OWN), copies(CHUNKS, UNITS),
            copies(2), copies(2),
            copies(UNITS), copies(OWN),
            copies(OWN), copies(UNITS),
            copies(OWN), copies(OWN),
            copies(OWN), copies(OWN),
        ],
        compiler_params=pltpu.CompilerParams(collective_id=0, has_side_effects=True, vmem_limit_bytes=48 << 20),
        name="exchange_attention",
    )(*operands)

    kv_shape = (TOK_DEV, KEY_HEADS * HEAD_WIDTH)
    shapes = ((queries.shape, BF16), (queries.shape, F32), (kv_shape, F32), (kv_shape, F32))
    return pl.pallas_call(
        unpack_kernel,
        out_shape=tuple(jax.ShapeDtypeStruct(*s) for s in shapes),
        in_specs=[pl.BlockSpec(memory_space=pltpu.VMEM)] * 3,
        out_specs=(pl.BlockSpec(memory_space=pltpu.HBM),) * 4,
        scratch_shapes=[pltpu.VMEM(*s) for s in shapes] + [pltpu.SemaphoreType.DMA((18,))],
        compiler_params=pltpu.CompilerParams(vmem_limit_bytes=32 << 20),
        name="rows_to_loader_order",
    )(ret, retkv, place)


def solution(mesh):
    rows = P(("dp", "ctx"), None)
    return jax.shard_map(
        local, mesh=mesh, in_specs=(rows,) * 5 + (P("dp", None),), out_specs=(rows,) * 4, check_vma=False
    )
```

time: 82.1 us -> 67.5 us (0.82)
  local copies, waits for them, and re-layouts: 7.63 us -> 0 us
  Pallas kernels: 73.4 us -> 66.7 us
    unnamed x16 -> x0, local copies, waits for them, and re-layouts: 7.63 us -> none
    pallas_call x2, Pallas kernels: 73.4 us -> 66.7 us  [the longest x1 64.4 us: local(): pl.pallas_call(main_kernel, out_shape=(jax.ShapeDtypeStruct(out_rows.shap...]
where the time goes in v2:
time: 67.5 us; the launch traced here: 67.3 us
  Pallas kernels  66.7 us (99%)
    pallas_call x1, Pallas kernels, local(): pl.pallas_call(main_kernel, out_shape=(jax.ShapeDtypeStruct(out_rows.shap...  64.4 us
    pallas_call x1, Pallas kernels, local(): pl.pallas_call(unpack_kernel, out_shape=tuple((jax.ShapeDtypeStruct(*s) f...  2.29 us

profile of v2, /device:TPU:1, one launch (start us, length us, event | category | flops | bytes accessed | tf_op | source)
XLA Modules:
  0.0 67.3 jit_solution(384107760820943735)
XLA Ops:
  0.6 64.4 %exchange_attention.1 = (bf16[2,4,16,64,128]{4,3,2,1,0:T(8,128)(2,1)S(1)}, bf16[4,16,16,128]{3,2,1,0:T(8,128)(2,1)S(1)}, bf16[256,256]{1,0:T(8,128)(2,1)S(1)}) custom-call(bf16[128,4096]{1,0:T(8,128)(2,1)} %q_hbm.1, bf16[128,512]{1,0:T(8,128)(2,1)} %k_hbm.1, bf16[128,512]{1,0:T(8,128)(2,1)} %v_hbm.1, bf16[128,4096]{1,0:T(8,128)(2,1)} %d_hbm.1, ...), custom_call_target="tpu_custom_call" | custom-call | tf_op jit(solution)/shard_map/exchange_attention/pallas_call | solution.py:432
  65.0 2.3 %rows_to_loader_order.1 = (bf16[128,4096]{1,0:T(8,128)(2,1)}, f32[128,4096]{1,0:T(8,128)}, f32[128,512]{1,0:T(8,128)}, f32[128,512]{1,0:T(8,128)}) custom-call(bf16[2,4,16,64,128]{4,3,2,1,0:T(8,128)(2,1)S(1)} %get-tuple-element.7.ret, bf16[4,16,16,128]{3,2,1,0:T(8,128)(2,1)S(1)} %get-tuple-element.8.retkv, bf16[256,256]{1,0:T(8,128)(2,1)S(1)} %get-tuple-element.9.place), custom_call_target="tpu_custom_call" | custom-call | tf_op jit(solution)/shard_map/rows_to_loader_order/pallas_call | solution.py:481

commit v3 on v2

--- a/solution.py
+++ b/solution.py
@@ -151,19 +151,20 @@
 
     load_kv[1].wait()
     load_kv[2].wait()
+    k_rows, v_rows = dot_nn(picks, k_in[...]), dot_nn(picks, v_in[...])
     for u in range(UNITS):
         cols = slice(u * HEAD_WIDTH, (u + 1) * HEAD_WIDTH)
-        kvsend[u] = pair_rows(dot_nn(picks, k_in[:, cols]), dot_nn(picks, v_in[:, cols]))
+        kvsend[u] = pair_rows(k_rows[:, cols], v_rows[:, cols])
 
     def pack_chunk(ch):
         wait_bytes(q_in.at[:, pl.ds(0, UNITS * part_wide)], load_sem.at[4 + 2 * ch])
         wait_bytes(d_in.at[:, pl.ds(0, UNITS * part_wide)], load_sem.at[5 + 2 * ch])
         for u in range(UNITS):
+            wide = slice((u * CHUNKS + ch) * part_wide, (u * CHUNKS + ch + 1) * part_wide)
+            q_rows, d_rows = dot_nn(picks, q_in[:, wide]), dot_nn(picks, d_in[:, wide])
             for h in range(CHUNK_HEADS):
-                head = (u * CHUNKS + ch) * CHUNK_HEADS + h
-                cols = slice(head * HEAD_WIDTH, (head + 1) * HEAD_WIDTH)
-                tile = pair_rows(dot_nn(picks, q_in[:, cols]), dot_nn(picks, d_in[:, cols]))
-                send[ch, u, :, h * 16 : (h + 1) * 16] = tile
+                cols = slice(h * HEAD_WIDTH, (h + 1) * HEAD_WIDTH)
+                send[ch, u, :, h * 16 : (h + 1) * 16] = pair_rows(q_rows[:, cols], d_rows[:, cols])
 
     pack_chunk(0)
     pl.semaphore_wait(barrier, 3 * (PLANE - 1))
@@ -395,19 +396,20 @@
     head = 0
     for u in range(UNITS):
         for ch in range(CHUNKS):
-            for h in range(CHUNK_HEADS):
-                rows = ret[ch, u, :, h * 16 : (h + 1) * 16].reshape(2 * DEVICES, HEAD_WIDTH)
-                both = dot_nn(place[...], rows)
-                cols = slice(head * HEAD_WIDTH, (head + 1) * HEAD_WIDTH)
+            for h in range(0, CHUNK_HEADS, 2):
+                rows = [ret[ch, u, :, n * 16 : (n + 1) * 16].reshape(2 * DEVICES, HEAD_WIDTH) for n in (h, h + 1)]
+                both = dot_nn(place[...], jnp.concatenate(rows, axis=1))
+                cols = slice(head * HEAD_WIDTH, (head + 2) * HEAD_WIDTH)
                 out_s[:, cols] = both[:TOK_DEV].astype(BF16)
                 gq_s[:, cols] = both[TOK_DEV:]
-                head += 1
+                head += 2
             wide = CHUNK_HEADS * HEAD_WIDTH
             put(out_s, out, pl.ds((u * CHUNKS + ch) * wide, wide))
             put(gq_s, gq, pl.ds((u * CHUNKS + ch) * wide, wide))
-    for u in range(UNITS):
-        cols = slice(u * HEAD_WIDTH, (u + 1) * HEAD_WIDTH)
-        both = dot_nn(place[...], retkv[u].reshape(2 * DEVICES, HEAD_WIDTH))
+    for u in range(0, UNITS, 2):
+        cols = slice(u * HEAD_WIDTH, (u + 2) * HEAD_WIDTH)
+        rows = [retkv[n].reshape(2 * DEVICES, HEAD_WIDTH) for n in (u, u + 1)]
+        both = dot_nn(place[...], jnp.concatenate(rows, axis=1))
         gk_s[:, cols] = both[:TOK_DEV]
         gv_s[:, cols] = both[TOK_DEV:]
     put(gk_s, gk, pl.ds(0, KEY_HEADS * HEAD_WIDTH))

time: 67.5 us -> 67.2 us (level)
  no operation moved by 1% of the time
where the time goes in v3:
time: 67.2 us; the launch traced here: 67.1 us
  Pallas kernels  66.4 us (99%)
    pallas_call x1, Pallas kernels, local(): pl.pallas_call(main_kernel, out_shape=(jax.ShapeDtypeStruct(out_rows.shap...  64.3 us
    pallas_call x1, Pallas kernels, local(): pl.pallas_call(unpack_kernel, out_shape=tuple((jax.ShapeDtypeStruct(*s) f...  2.18 us

profile of v3, /device:TPU:1, one launch (start us, length us, event | category | flops | bytes accessed | tf_op | source)
XLA Modules:
  0.0 67.1 jit_solution(3742789105878621516)
XLA Ops:
  0.6 64.3 %exchange_attention.1 = (bf16[2,4,16,64,128]{4,3,2,1,0:T(8,128)(2,1)S(1)}, bf16[4,16,16,128]{3,2,1,0:T(8,128)(2,1)S(1)}, bf16[256,256]{1,0:T(8,128)(2,1)S(1)}) custom-call(bf16[128,4096]{1,0:T(8,128)(2,1)} %q_hbm.1, bf16[128,512]{1,0:T(8,128)(2,1)} %k_hbm.1, bf16[128,512]{1,0:T(8,128)(2,1)} %v_hbm.1, bf16[128,4096]{1,0:T(8,128)(2,1)} %d_hbm.1, ...), custom_call_target="tpu_custom_call" | custom-call | tf_op jit(solution)/shard_map/exchange_attention/pallas_call | solution.py:434
  64.9 2.2 %rows_to_loader_order.1 = (bf16[128,4096]{1,0:T(8,128)(2,1)}, f32[128,4096]{1,0:T(8,128)}, f32[128,512]{1,0:T(8,128)}, f32[128,512]{1,0:T(8,128)}) custom-call(bf16[2,4,16,64,128]{4,3,2,1,0:T(8,128)(2,1)S(1)} %get-tuple-element.7.ret, bf16[4,16,16,128]{3,2,1,0:T(8,128)(2,1)S(1)} %get-tuple-element.8.retkv, bf16[256,256]{1,0:T(8,128)(2,1)S(1)} %get-tuple-element.9.place), custom_call_target="tpu_custom_call" | custom-call | tf_op jit(solution)/shard_map/rows_to_loader_order/pallas_call | solution.py:483

commit v4 on v3

--- a/solution.py
+++ b/solution.py
@@ -211,14 +211,18 @@
             to = peer(kind, (plane[kind] + d) % 4)
             remote(block, block, fws_sem.at[u % OWN], fwr_sem.at[u % OWN], to).start()
 
+    def drained(ch, w):
+        for u in range(w, UNITS, OWN):
+            wait_bytes(send.at[ch, u, pl.ds(0, 15)], in_send.at[ch, u])
+            pl.when(core != u // OWN)(lambda u=u: wait_bytes(send.at[ch, u, 0], in_send.at[ch, u]))
+
     send_chunk(0, 0)
     pack_chunk(1)
     for w in range(OWN):
         wait_bytes(kv.at[w, 0], kvr_sem.at[w])
         for_own(w, hand_on)
+    drained(0, 0)
     send_chunk(0, 1)
-    send_chunk(1, 0)
-    send_chunk(1, 1)
 
     goes = lax.broadcasted_iota(jnp.int32, (DEVICES, 2 * DEVICES), 0)
     lane = lax.broadcasted_iota(jnp.int32, (DEVICES, 2 * DEVICES), 1)
@@ -338,6 +342,9 @@
             pl.when(w == own)(lambda own=own: for_own(own, return_rows))
         return carry
 
+    drained(0, 1)
+    send_chunk(1, 0)
+    send_chunk(1, 1)
     lax.fori_loop(0, CHUNKS * OWN, one_step, 0)
 
     def return_kv(u, kind):
@@ -363,14 +370,11 @@
     for u in range(UNITS):
         for ch in range(CHUNKS):
             wait_bytes(ret.at[ch, u], out_recv.at[ch, u])
-            wait_bytes(send.at[ch, u, pl.ds(0, 15)], in_send.at[ch, u])
         wait_bytes(retkv.at[u], kr_sem.at[u])
         wait_bytes(kvsend.at[u, pl.ds(0, 15)], kvs_sem.at[u])
 
         @pl.when(core != u // OWN)
         def _():
-            for ch in range(CHUNKS):
-                wait_bytes(send.at[ch, u, 0], in_send.at[ch, u])
             wait_bytes(kvsend.at[u, 0], kvs_sem.at[u])
 
     for w in range(OWN):
@@ -379,6 +383,8 @@
         wait_bytes(kv.at[w, pl.ds(0, 3)], fws_sem.at[w])
         wait_bytes(pxs.at[w, pl.ds(0, 3)], pxs_sem.at[w])
         wait_bytes(kvout.at[w, pl.ds(0, PLANE - 1)], ks_sem.at[w])
+    drained(1, 0)
+    drained(1, 1)
     for kind in (Z, Y):
 
         @pl.when(jnp.logical_not(doc_stays[kind]))

time: 67.2 us -> 67.6 us (level)
  no operation moved by 1% of the time
where the time goes in v4:
time: 67.6 us; the launch traced here: 67.4 us
  Pallas kernels  66.8 us (99%)
    pallas_call x1, Pallas kernels, local(): pl.pallas_call(main_kernel, out_shape=(jax.ShapeDtypeStruct(out_rows.shap...  64.6 us
    pallas_call x1, Pallas kernels, local(): pl.pallas_call(unpack_kernel, out_shape=tuple((jax.ShapeDtypeStruct(*s) f...  2.18 us

profile of v4, /device:TPU:1, one launch (start us, length us, event | category | flops | bytes accessed | tf_op | source)
XLA Modules:
  0.0 67.4 jit_solution(14659188389687975651)
XLA Ops:
  0.6 64.6 %exchange_attention.1 = (bf16[2,4,16,64,128]{4,3,2,1,0:T(8,128)(2,1)S(1)}, bf16[4,16,16,128]{3,2,1,0:T(8,128)(2,1)S(1)}, bf16[256,256]{1,0:T(8,128)(2,1)S(1)}) custom-call(bf16[128,4096]{1,0:T(8,128)(2,1)} %q_hbm.1, bf16[128,512]{1,0:T(8,128)(2,1)} %k_hbm.1, bf16[128,512]{1,0:T(8,128)(2,1)} %v_hbm.1, bf16[128,4096]{1,0:T(8,128)(2,1)} %d_hbm.1, ...), custom_call_target="tpu_custom_call" | custom-call | tf_op jit(solution)/shard_map/exchange_attention/pallas_call | solution.py:440
  65.3 2.2 %rows_to_loader_order.1 = (bf16[128,4096]{1,0:T(8,128)(2,1)}, f32[128,4096]{1,0:T(8,128)}, f32[128,512]{1,0:T(8,128)}, f32[128,512]{1,0:T(8,128)}) custom-call(bf16[2,4,16,64,128]{4,3,2,1,0:T(8,128)(2,1)S(1)} %get-tuple-element.7.ret, bf16[4,16,16,128]{3,2,1,0:T(8,128)(2,1)S(1)} %get-tuple-element.8.retkv, bf16[256,256]{1,0:T(8,128)(2,1)S(1)} %get-tuple-element.9.place), custom_call_target="tpu_custom_call" | custom-call | tf_op jit(solution)/shard_map/rows_to_loader_order/pallas_call | solution.py:489

commit v5 on v4

--- a/solution.py
+++ b/solution.py
@@ -221,7 +221,6 @@
     for w in range(OWN):
         wait_bytes(kv.at[w, 0], kvr_sem.at[w])
         for_own(w, hand_on)
-    drained(0, 0)
     send_chunk(0, 1)
 
     goes = lax.broadcasted_iota(jnp.int32, (DEVICES, 2 * DEVICES), 0)
@@ -342,7 +341,7 @@
             pl.when(w == own)(lambda own=own: for_own(own, return_rows))
         return carry
 
-    drained(0, 1)
+    drained(0, 0)
     send_chunk(1, 0)
     send_chunk(1, 1)
     lax.fori_loop(0, CHUNKS * OWN, one_step, 0)
@@ -383,6 +382,7 @@
         wait_bytes(kv.at[w, pl.ds(0, 3)], fws_sem.at[w])
         wait_bytes(pxs.at[w, pl.ds(0, 3)], pxs_sem.at[w])
         wait_bytes(kvout.at[w, pl.ds(0, PLANE - 1)], ks_sem.at[w])
+    drained(0, 1)
     drained(1, 0)
     drained(1, 1)
     for kind in (Z, Y):

time: 67.6 us -> 66.9 us (0.990)
  Pallas kernels: 66.8 us -> 66.1 us
    pallas_call x1, Pallas kernels: 64.6 us -> 63.9 us  [local(): pl.pallas_call(main_kernel, out_shape=(jax.ShapeDtypeStruct(out_rows.shap...]
where the time goes in v5:
time: 66.9 us; the launch traced here: 66.7 us
  Pallas kernels  66.1 us (99%)
    pallas_call x1, Pallas kernels, local(): pl.pallas_call(main_kernel, out_shape=(jax.ShapeDtypeStruct(out_rows.shap...  63.9 us
    pallas_call x1, Pallas kernels, local(): pl.pallas_call(unpack_kernel, out_shape=tuple((jax.ShapeDtypeStruct(*s) f...  2.18 us

profile of v5, /device:TPU:1, one launch (start us, length us, event | category | flops | bytes accessed | tf_op | source)
XLA Modules:
  0.0 66.7 jit_solution(3425625040930061846)
XLA Ops:
  0.6 63.9 %exchange_attention.1 = (bf16[2,4,16,64,128]{4,3,2,1,0:T(8,128)(2,1)S(1)}, bf16[4,16,16,128]{3,2,1,0:T(8,128)(2,1)S(1)}, bf16[256,256]{1,0:T(8,128)(2,1)S(1)}) custom-call(bf16[128,4096]{1,0:T(8,128)(2,1)} %q_hbm.1, bf16[128,512]{1,0:T(8,128)(2,1)} %k_hbm.1, bf16[128,512]{1,0:T(8,128)(2,1)} %v_hbm.1, bf16[128,4096]{1,0:T(8,128)(2,1)} %d_hbm.1, ...), custom_call_target="tpu_custom_call" | custom-call | tf_op jit(solution)/shard_map/exchange_attention/pallas_call | solution.py:440
  64.5 2.2 %rows_to_loader_order.1 = (bf16[128,4096]{1,0:T(8,128)(2,1)}, f32[128,4096]{1,0:T(8,128)}, f32[128,512]{1,0:T(8,128)}, f32[128,512]{1,0:T(8,128)}) custom-call(bf16[2,4,16,64,128]{4,3,2,1,0:T(8,128)(2,1)S(1)} %get-tuple-element.7.ret, bf16[4,16,16,128]{3,2,1,0:T(8,128)(2,1)S(1)} %get-tuple-element.8.retkv, bf16[256,256]{1,0:T(8,128)(2,1)S(1)} %get-tuple-element.9.place), custom_call_target="tpu_custom_call" | custom-call | tf_op jit(solution)/shard_map/rows_to_loader_order/pallas_call | solution.py:489
